TPU v7x, 256 devices: a whole 4x4x8 slice. The times are simulated.
256 devices in a mesh: dp: 2 (over y_hi), expert: 128 (over z, x, y_lo, core).
Axes of the slice: x: 4, y: 4 (y_hi: 2, y_lo: 2; y = y_hi * 2 + y_lo), z: 8, core: 2. Of those that a mesh axis runs over, the one named last changes fastest.
Arguments:
- tokens: bfloat16 [4096, 2880], P(('dp', 'expert')), may hold values from -6 to 6
- grad_out: bfloat16 [4096, 2880], P(('dp', 'expert')), may hold values from -6 to 6
- route_ids: int32 [4096, 4], P(('dp', 'expert')), may hold values from 0 to 39, all different within a row; in each aligned block of 16 rows (0 to 15, 16 to 31, ...) at most 2 rows name the same one
- route_prob: float32 [4096, 4], P(('dp', 'expert')), may hold values from 0.05 to 1
- device_expert: int32 [128], replicated, may hold values from 0 to 39, as said below
- unit_count: int32 [128], replicated, may hold values from 264 to 480, as said below
- expert_weights: bfloat16 [128, 480, 8640], P('expert'), may hold values from -0.109375 to 0.109375
Outputs:
- grad_tokens: bfloat16 [4096, 2880], P(('dp', 'expert'))
- grad_weights: bfloat16 [128, 480, 8640], P('expert', 'dp')
Inputs may be any that keep to these rules, and one draw needn't show every extreme that they name: `route_ids`: each row names 4 different experts; the 16 rows of one device name each expert at most 2 times, and in every draw some device names some expert exactly 2 times. `device_expert`: aligned blocks of 16 indices of expert hold 5 experts, ids rising by one from 5 times the block's number; the indices of one expert are consecutive, 3 or 4 of them; every expert has a group. `unit_count`: the counts of the indices of one expert sum to 1440; rows of expert_weights at or past a slot's count are not part of the model.
All inputs are finite; a program needn't handle non-finite values.
Results may differ from a plain program's by a relative error of at most 0.0058.
Values may be sent and summed in bfloat16 or wider, within the bound.
No kernel may reach another device: no remote copies, remote signals or barrier semaphores. Data moves between devices by JAX's collectives and lax.ppermute only.
A program may use at most 128 MiB of HBM per device.

v0:
```python
import jax
import jax.numpy as jnp
from jax import lax
from jax.sharding import PartitionSpec as P


def silu_parts(preact):
    sigma = jax.nn.sigmoid(preact)
    return (preact * sigma, sigma * (1.0 + preact * (1.0 - sigma)))


def unit_work(token_rows, grad_rows, slot_weights, unit_mask):
    width = token_rows.shape[1]
    gate_rows = slot_weights[:, :width]
    up_rows = slot_weights[:, width : 2 * width]
    down_rows = slot_weights[:, 2 * width :]
    contract = (((1,), (1,)), ((), ()))
    gate_pre = lax.dot_general(token_rows, gate_rows, contract, preferred_element_type=jnp.float32)
    up_pre = lax.dot_general(token_rows, up_rows, contract, preferred_element_type=jnp.float32)
    back_grad = lax.dot_general(grad_rows, down_rows, contract, preferred_element_type=jnp.float32)
    active, slope = silu_parts(gate_pre)
    hidden = (active * up_pre * unit_mask).astype(jnp.bfloat16)
    grad_gate = (back_grad * up_pre * slope * unit_mask).astype(jnp.bfloat16)
    grad_up = (back_grad * active * unit_mask).astype(jnp.bfloat16)
    partial_value = jnp.dot(grad_gate, gate_rows, preferred_element_type=jnp.float32) + jnp.dot(
        grad_up, up_rows, preferred_element_type=jnp.float32
    )
    return (partial_value, hidden, grad_gate, grad_up)


def weight_terms(token_rows, grad_rows, hidden, grad_gate, grad_up):
    rows_first = (((0,), (0,)), ((), ()))
    return jnp.concatenate(
        [
            lax.dot_general(grad_gate, token_rows, rows_first, preferred_element_type=jnp.float32),
            lax.dot_general(grad_up, token_rows, rows_first, preferred_element_type=jnp.float32),
            lax.dot_general(hidden, grad_rows, rows_first, preferred_element_type=jnp.float32),
        ],
        axis=1,
    )


def send_back(partial_value):
    return lax.all_to_all(partial_value, "expert", split_axis=0, concat_axis=0, tiled=True)


def shards(tokens, grad_out, route_ids, route_prob, device_expert, unit_count, expert_weights):
    token_count, width = tokens.shape
    top_count = route_ids.shape[1]
    devices = lax.axis_size("expert")
    experts = 5 * devices // 16
    capacity = token_count * top_count * 4 // devices
    flat_ids = route_ids.reshape(-1)
    onehot = (flat_ids[:, None] == jnp.arange(experts, dtype=jnp.int32)[None, :]).astype(jnp.int32)
    rank_of = jnp.sum(onehot * jnp.cumsum(onehot, axis=0), axis=1) - 1
    picked = (flat_ids[None, None, :] == device_expert[:, None, None]) & (
        rank_of[None, None, :] == jnp.arange(capacity, dtype=jnp.int32)[None, :, None]
    )
    picked = picked.astype(jnp.float32).reshape(devices * capacity, token_count * top_count)
    by_token = picked.reshape(devices * capacity, token_count, top_count).sum(axis=2)
    route_scale = jnp.dot(picked, route_prob.reshape(-1), precision=lax.Precision.HIGHEST)
    by_token_low = by_token.astype(jnp.bfloat16)
    sent_rows = jnp.dot(by_token_low, tokens, preferred_element_type=jnp.float32).astype(
        jnp.bfloat16
    )
    sent_grads = (
        route_scale[:, None] * jnp.dot(by_token_low, grad_out, preferred_element_type=jnp.float32)
    ).astype(jnp.bfloat16)
    outgoing = jnp.stack([sent_rows, sent_grads], axis=1).reshape(devices, capacity, 2, width)
    position = lax.axis_index("expert")
    unit_limit = lax.dynamic_index_in_dim(unit_count, position, keepdims=False)
    slot_weights = expert_weights[0]
    slot_units = slot_weights.shape[0]
    unit_mask = (jnp.arange(slot_units, dtype=jnp.int32) < unit_limit).astype(jnp.float32)
    arrived = lax.all_to_all(outgoing, "expert", split_axis=0, concat_axis=0, tiled=True)
    row_pairs = arrived.reshape(-1, 2, width)
    partial_value, hidden, grad_gate, grad_up = unit_work(
        row_pairs[:, 0], row_pairs[:, 1], slot_weights, unit_mask
    )
    leading = (arrived.shape[0], arrived.shape[1])
    returned, all_rows, hidden, grad_gate, grad_up = (
        send_back(partial_value.reshape(leading + (width,))),
        arrived,
        hidden.reshape(leading + (slot_units,)),
        grad_gate.reshape(leading + (slot_units,)),
        grad_up.reshape(leading + (slot_units,)),
    )
    row_pairs = all_rows.reshape(-1, 2, width)
    token_rows = row_pairs[:, 0]
    grad_rows = row_pairs[:, 1]
    hidden = hidden.reshape(-1, slot_units)
    grad_gate = grad_gate.reshape(-1, slot_units)
    grad_up = grad_up.reshape(-1, slot_units)
    term_block = weight_terms(token_rows, grad_rows, hidden, grad_gate, grad_up)
    grad_weights = lax.psum_scatter(term_block, "dp", scatter_dimension=0, tiled=True)
    parts = returned.reshape(devices * capacity, width)
    grad_tokens = lax.dot_general(
        by_token,
        parts,
        (((0,), (0,)), ((), ())),
        precision=lax.Precision.HIGHEST,
        preferred_element_type=jnp.float32,
    )
    return (grad_tokens.astype(jnp.bfloat16), grad_weights.astype(jnp.bfloat16)[None])


def solution(mesh):
    in_specs = (
        P(("dp", "expert"), None),
        P(("dp", "expert"), None),
        P(("dp", "expert"), None),
        P(("dp", "expert"), None),
        P(),
        P(),
        P("expert", None, None),
    )
    out_specs = (P(("dp", "expert"), None), P("expert", "dp", None))
    return jax.shard_map(shards, mesh=mesh, in_specs=in_specs, out_specs=out_specs, check_vma=False)
```

profile of v0, /device:TPU:2, one launch (start us, length us, event | category | flops | bytes accessed | tf_op | source)
XLA Modules:
  0.0 412.8 jit_solution(8017211491969790921)
XLA Ops:
  17.0 3.3 stack.9
  20.3 4.4 %pad_maximum_fusion = bf16[128,2,2,2880]{3,1,0,2:T(2,128)(2,1)S(1)} fusion(bf16[128,2,1,2880]{3,1,0,2:T(2,128)(2,1)S(1)} %stack.10, bf16[128,2,1,2880]{3,1,0,2:T(2,128)(2,1)S(1)} %stack.9), kind=kLoop, calls=%fused_computation.6 | loop fusion | flops 1474560 | bytes 5898240 | tf_op jit(solution)/shard_map/stack | solution.py:69
  24.7 3.7 copy.29
  28.4 13.9 %all-to-all-start = ((bf16[128,2,2,2880]{3,1,2,0:T(2,128)(2,1)}), bf16[128,2,2,2880]{3,1,2,0:T(2,128)(2,1)S(1)}, u32[]{:S(2)}, u32[]{:S(2)}) async-start(bf16[128,2,2,2880]{3,1,2,0:T(2,128)(2,1)} %copy.29), calls=%async_computation | async-start | bytes 6029312 | tf_op jit(solution)/shard_map/all_to_all | solution.py:75
  43.9 68.3 %all-to-all-done = bf16[128,2,2,2880]{3,1,2,0:T(2,128)(2,1)S(1)} async-done(((bf16[128,2,2,2880]{3,1,2,0:T(2,128)(2,1)}), bf16[128,2,2,2880]{3,1,2,0:T(2,128)(2,1)S(1)}, u32[]{:S(2)}, u32[]{:S(2)}) %all-to-all-start) | async-done | bytes 2949152 | tf_op jit(solution)/shard_map/all_to_all | solution.py:75
  112.2 2.4 copy.30
  114.6 5.7 %fusion.28 = (bf16[256,1,2880]{2,1,0:T(2,128)(2,1)}, bf16[256,1,2880]{2,1,0:T(2,128)(2,1)}) fusion(bf16[256,2,2880]{2,1,0:T(2,128)(2,1)S(1)} %bitcast.32), kind=kLoop, calls=%fused_computation.44 | loop fusion | bytes 5898240 | tf_op jit(solution)/shard_map/slice | solution.py:78
  120.3 6.8 %copy.32 = bf16[256,1,2880]{0,2,1:T(8,128)(2,1)S(1)} copy(bf16[256,1,2880]{2,1,0:T(2,128)(2,1)} %get-tuple-element.3) | data formatting | bytes 2949120 | tf_op jit(solution)/shard_map/slice | solution.py:78
  127.1 3.9 fusion.8
  131.0 3.5 fusion.5
  134.5 6.8 %copy.31 = bf16[256,1,2880]{0,2,1:T(8,128)(2,1)S(1)} copy(bf16[256,1,2880]{2,1,0:T(2,128)(2,1)} %get-tuple-element.2) | data formatting | bytes 2949120 | tf_op jit(solution)/shard_map/slice | solution.py:78
  141.3 3.1 multiply_convert_fusion.1
  144.5 3.4 fusion.16
  147.9 3.5 fusion.10
  151.3 3.4 fusion.12
  154.8 19.8 %concatenate.4 = f32[480,8640]{1,0:T(8,128)} concatenate(f32[480,2880]{1,0:T(8,128)} %fusion.12, f32[480,2880]{1,0:T(8,128)} %fusion.10, f32[480,2880]{1,0:T(8,128)} %fusion.16), dimensions={1} | concatenate | bytes 33177600 | tf_op jit(solution)/shard_map/concatenate | solution.py:33
  175.6 3.1 fusion.3
  178.7 6.4 %convolution_add_fusion = f32[256,2880]{0,1:T(8,128)} fusion(f32[256,2880]{0,1:T(8,128)S(1)} %fusion.3, bf16[256,480]{0,1:T(8,128)(2,1)S(1)} %get-tuple-element.4, bf16[480,8640]{1,0:T(8,128)(2,1)} %bitcast.37), kind=kOutput, calls=%fused_computation.1 | convolution fusion | flops 708526080 | bytes 8970240 | tf_op jit(solution)/shard_map/dot_general | solution.py:25
  185.1 2.3 copy.33
  187.4 3.2 reshape.107
  190.6 78.9 %all_to_all.10 = f32[128,2,2880]{2,1,0:T(2,128)} all-to-all(f32[128,2,2880]{2,1,0:T(2,128)} %reshape.107), channel_id=1, replica_groups=mesh['dp'=2,'expert'=128] {'expert'}, dimensions={0} | all-to-all | bytes 5898240 | tf_op jit(solution)/shard_map/all_to_all | solution.py:44
  269.5 3.7 reshape.108
  275.4 124.7 %reduce-scatter.2.cloned.1.call-done = f32[240,8640]{1,0:T(8,128)} async-done(((f32[480,8640]{1,0:T(8,128)}), f32[240,8640]{1,0:T(8,128)}) %reduce-scatter.2.cloned.1.call-update) | async-done | bytes 8294416 | tf_op jit(solution)/shard_map/reduce_scatter | solution.py:95
  400.2 5.8 %convert_bitcast_fusion = bf16[1,240,8640]{2,1,0:T(8,128)(2,1)} fusion(f32[240,8640]{1,0:T(8,128)} %reduce-scatter.2.cloned.1.call-done), kind=kLoop, calls=%fused_computation | loop fusion | flops 2073600 | bytes 12441600 | tf_op jit(solution)/shard_map/broadcast_in_dim | solution.py:104
  (41 shorter events, 14.3 us)
Async XLA Ops:
  7.2 5.1 %copy-start = (bf16[16,2880]{1,0:T(8,128)(2,1)S(1)}, bf16[16,2880]{1,0:T(8,128)(2,1)}, u32[]{:S(2)}) copy-start(bf16[16,2880]{1,0:T(8,128)(2,1)} %param.8) | copy-start | bytes 276484
  12.8 1.8 copy-start.6
  28.4 14.2 %copy-start.7 = (s32[128]{0:T(128)S(1)}, s32[128]{0:T(128)}, u32[]{:S(2)}) copy-start(s32[128]{0:T(128)} %param.12) | copy-start | bytes 1540
  28.4 83.8 %all-to-all-start = ((bf16[128,2,2,2880]{3,1,2,0:T(2,128)(2,1)}), bf16[128,2,2,2880]{3,1,2,0:T(2,128)(2,1)S(1)}, u32[]{:S(2)}, u32[]{:S(2)}) async-start(bf16[128,2,2,2880]{3,1,2,0:T(2,128)(2,1)} %copy.29), calls=%async_computation | async-start | bytes 6029312 | tf_op jit(solution)/shard_map/all_to_all | solution.py:75
  42.4 357.8 %reduce-scatter.2.cloned.1.call-start = ((), (), s32[]{:S(2)}) async-start(), calls=%async_computation.3 | async-start | bytes 25067520 | tf_op jit(solution)/shard_map/reduce_scatter | solution.py:95
  141.3 3.2 copy-start.4
  141.3 3.2 copy-start.5
  144.4 6.9 %copy-start.2 = (bf16[256,480]{0,1:T(8,128)(2,1)}, bf16[256,480]{0,1:T(8,128)(2,1)S(1)}, u32[]{:S(2)}) copy-start(bf16[256,480]{0,1:T(8,128)(2,1)S(1)} %get-tuple-element.5) | copy-start | bytes 737284
  174.6 0.9 copy-start.3
  400.2 5.8 %copy-start.1 = (bf16[16,2880]{1,0:T(8,128)(2,1)S(1)}, bf16[16,2880]{1,0:T(8,128)(2,1)}, u32[]{:S(2)}) copy-start(bf16[16,2880]{1,0:T(8,128)(2,1)} %param.8) | copy-start | bytes 276484
Sparse Core Ops, SparseCore 0:
  174.8 225.3 reduce-scatter.1
where the time goes:
time: 415 us; the launch traced here: 413 us
  waiting for transfers between devices  193 us (47%)
  blocking collectives  78.9 us (19%)
  local copies, waits for them, and re-layouts  65.7 us (16%)
  matrix products  33.9 us (8%)
  between operations  14.3 us (3%)
  starting transfers between devices  14.2 us (3%)
  other arithmetic  12.8 us (3%)
    reduce_scatter x1, waiting for transfers between devices, shards(): lax.psum_scatter(term_block, 'dp', scatter_dimension=0, tiled=True)  125 us
    all_to_all x1, blocking collectives, send_back(): lax.all_to_all(partial_value, 'expert', split_axis=0, concat_axis=0, tile...  78.9 us
    all_to_all x1, waiting for transfers between devices, shards(): lax.all_to_all(outgoing, 'expert', split_axis=0, concat_axis=0, tiled=True)  68.3 us
    concatenate x1, local copies, waits for them, and re-layouts, weight_terms(): jnp.concatenate([lax.dot_general(grad_gate, token_rows, rows_first, prefe...  19.8 us
    all_to_all x1, starting transfers between devices, shards(): lax.all_to_all(outgoing, 'expert', split_axis=0, concat_axis=0, tiled=True)  13.9 us
    slice x2, local copies, waits for them, and re-layouts, shards(): row_pairs[:, 1]  12.5 us
  transfers between devices with their start and end apart: 2, of which 2 were waited for; matrix products, arithmetic and copies ran while one was open for 5% of the time, Pallas kernels for 0%

commit v1 on v0

v1 whole, which is shorter than its diff:
```python
import jax
import jax.numpy as jnp
from jax import lax
from jax.sharding import PartitionSpec as P

F32 = jnp.float32
BF16 = jnp.bfloat16


def dot(left, right, left_dim, right_dim):
    return lax.dot_general(
        left, right, (((left_dim,), (right_dim,)), ((), ())), preferred_element_type=F32
    )


def swap_dp(value):
    return lax.ppermute(value, "dp", [(0, 1), (1, 0)])


def shards(tokens, grad_out, route_ids, route_prob, device_expert, unit_count, expert_weights):
    token_count, width = tokens.shape
    top_count = route_ids.shape[1]
    devices = lax.axis_size("expert")
    capacity = token_count * top_count * 4 // devices
    flat_ids = route_ids.reshape(-1)
    routes = jnp.arange(flat_ids.shape[0], dtype=jnp.int32)
    earlier = (flat_ids[:, None] == flat_ids[None, :]) & (routes[None, :] < routes[:, None])
    rank_of = jnp.sum(earlier.astype(jnp.int32), axis=1)
    picked = (flat_ids[None, None, :] == device_expert[:, None, None]) & (
        rank_of[None, None, :] == jnp.arange(capacity, dtype=jnp.int32)[None, :, None]
    )
    picked = picked.astype(F32).reshape(devices * capacity, token_count * top_count)
    by_token = picked.reshape(devices * capacity, token_count, top_count).sum(axis=2).astype(BF16)
    route_scale = jnp.sum(picked * route_prob.reshape(-1)[None, :], axis=1)
    sent_rows = dot(by_token, tokens, 1, 0).astype(BF16)
    sent_grads = (route_scale[:, None] * dot(by_token, grad_out, 1, 0)).astype(BF16)
    outgoing = jnp.stack(
        [
            sent_rows.reshape(devices, capacity, width),
            sent_grads.reshape(devices, capacity, width),
        ],
        axis=1,
    )
    arrived = lax.all_to_all(outgoing, "expert", split_axis=0, concat_axis=0, tiled=True)
    token_rows = arrived[:, 0].reshape(-1, width)
    grad_rows = arrived[:, 1].reshape(-1, width)
    other_token_rows = swap_dp(token_rows)
    other_grad_rows = swap_dp(grad_rows)

    position = lax.axis_index("expert")
    replica = lax.axis_index("dp")
    unit_limit = lax.dynamic_index_in_dim(unit_count, position, keepdims=False)
    slot_weights = expert_weights[0]
    slot_units = slot_weights.shape[0]
    unit_mask = (jnp.arange(slot_units, dtype=jnp.int32) < unit_limit).astype(F32)[:, None]
    gate_w = slot_weights[:, :width]
    up_w = slot_weights[:, width : 2 * width]
    down_w = slot_weights[:, 2 * width :]
    gate_pre = dot(gate_w, token_rows, 1, 1)
    up_pre = dot(up_w, token_rows, 1, 1)
    back_grad = dot(down_w, grad_rows, 1, 1)
    sigma = jax.nn.sigmoid(gate_pre)
    active = gate_pre * sigma
    slope = sigma * (1.0 + gate_pre * (1.0 - sigma))
    hidden = (active * up_pre * unit_mask).astype(BF16)
    grad_gate = (back_grad * up_pre * slope * unit_mask).astype(BF16)
    grad_up = (back_grad * active * unit_mask).astype(BF16)
    units = jnp.stack([grad_gate, grad_up, hidden])

    half = slot_units // 2
    own = lax.dynamic_slice_in_dim(units, replica * half, half, axis=1)
    other = swap_dp(lax.dynamic_slice_in_dim(units, (1 - replica) * half, half, axis=1))

    partial_value = (dot(grad_gate, gate_w, 0, 0) + dot(grad_up, up_w, 0, 0)).astype(BF16)
    returned = lax.all_to_all(
        partial_value.reshape(devices, capacity, width),
        "expert",
        split_axis=0,
        concat_axis=0,
        tiled=True,
    )
    grad_tokens = dot(by_token, returned.reshape(devices * capacity, width), 0, 0).astype(BF16)

    gate_up = dot(own[:2].reshape(2 * half, -1), token_rows, 1, 0) + dot(
        other[:2].reshape(2 * half, -1), other_token_rows, 1, 0
    )
    down = dot(own[2], grad_rows, 1, 0) + dot(other[2], other_grad_rows, 1, 0)
    grad_weights = jnp.concatenate(
        [gate_up[:half].astype(BF16), gate_up[half:].astype(BF16), down.astype(BF16)], axis=1
    )
    return grad_tokens, grad_weights[None]


def solution(mesh):
    in_specs = (
        P(("dp", "expert"), None),
        P(("dp", "expert"), None),
        P(("dp", "expert"), None),
        P(("dp", "expert"), None),
        P(),
        P(),
        P("expert", None, None),
    )
    out_specs = (P(("dp", "expert"), None), P("expert", "dp", None))
    return jax.shard_map(shards, mesh=mesh, in_specs=in_specs, out_specs=out_specs, check_vma=False)
```

time: 415 us -> 235 us (0.57)
  blocking collectives: 78.9 us -> 0 us
  waiting for transfers between devices: 193 us -> 121 us
  local copies, waits for them, and re-layouts: 65.7 us -> 47 us
  starting transfers between devices: 14.2 us -> 29 us
  between operations: 14.3 us -> 0.88 us
  matrix products: 33.9 us -> 27.3 us
  other arithmetic: 12.8 us -> 8.08 us
    reduce_scatter x1 -> x0, waiting for transfers between devices: 125 us -> none  [shards(): lax.psum_scatter(term_block, 'dp', scatter_dimension=0, tiled=True)]
    all_to_all x1 -> x0, blocking collectives: 78.9 us -> none  [send_back(): lax.all_to_all(partial_value, 'expert', split_axis=0, concat_axis=0, tile...]
    ppermute x0 -> x3, waiting for transfers between devices: none -> 52.5 us  [swap_dp(): return lax.ppermute(value, 'dp', [(0, 1), (1, 0)])]
    slice x3 -> x4, local copies, waits for them, and re-layouts: 19.2 us -> 4.63 us  [the longest x1 3.3 us: shards(): grad_rows = arrived[:, 1].reshape(-1, width)]
    concatenate x1, local copies, waits for them, and re-layouts: 19.8 us -> 7.43 us  [shards(): jnp.concatenate([gate_up[:half].astype(BF16), gate_up[half:].astype(BF16)...]
    another operation x3 -> x7, local copies, waits for them, and re-layouts: 7.65 us -> 17.8 us  [the longest x3 7.65 us: shards(): jnp.stack([sent_rows.reshape(devices, capacity, width), sent_grads.reshap...]
    all_to_all x0 -> x1, starting transfers between devices: none -> 8.57 us  [shards(): lax.all_to_all(partial_value.reshape(devices, capacity, width), 'expert',...]
    dot_general x12, matrix products: 33.9 us -> 27.3 us  [dot(): lax.dot_general(left, right, (((left_dim,), (right_dim,)), ((), ())), pre...]
  transfers between devices with their start and end apart: 2 -> 5, of which waited for: 2 -> 2; matrix products, arithmetic and copies ran while one was open for 5% -> 16% of each run, Pallas kernels for 0% -> 0%
where the time goes in v1:
time: 235 us; the launch traced here: 233 us
  waiting for transfers between devices  121 us (51%)
  local copies, waits for them, and re-layouts  47 us (20%)
  starting transfers between devices  29 us (12%)
  matrix products  27.3 us (12%)
  other arithmetic  8.08 us (3%)
    all_to_all x1, waiting for transfers between devices, shards(): lax.all_to_all(outgoing, 'expert', split_axis=0, concat_axis=0, tiled=True)  68.5 us
    ppermute x3, waiting for transfers between devices, swap_dp(): return lax.ppermute(value, 'dp', [(0, 1), (1, 0)])  52.5 us
    dot_general x12, matrix products, dot(): lax.dot_general(left, right, (((left_dim,), (right_dim,)), ((), ())), pre...  27.3 us
    all_to_all x1, starting transfers between devices, shards(): lax.all_to_all(outgoing, 'expert', split_axis=0, concat_axis=0, tiled=True)  13.9 us
    all_to_all x1, starting transfers between devices, shards(): lax.all_to_all(partial_value.reshape(devices, capacity, width), 'expert',...  8.57 us
    another operation x3, local copies, waits for them, and re-layouts, shards(): jnp.stack([sent_rows.reshape(devices, capacity, width), sent_grads.reshap...  7.65 us
    concatenate x1, local copies, waits for them, and re-layouts, shards(): jnp.concatenate([gate_up[:half].astype(BF16), gate_up[half:].astype(BF16)...  7.43 us
    ppermute x3, starting transfers between devices, swap_dp(): return lax.ppermute(value, 'dp', [(0, 1), (1, 0)])  6.52 us
  transfers between devices with their start and end apart: 5, of which 2 were waited for; matrix products, arithmetic and copies ran while one was open for 16% of the time, Pallas kernels for 0%

profile of v1, /device:TPU:2, one launch (start us, length us, event | category | flops | bytes accessed | tf_op | source)
XLA Modules:
  0.0 233.3 jit_solution(1529181755911214430)
XLA Ops:
  8.9 1.7 copy.25
  10.6 3.3 %stack_reshape.6 = bf16[128,1,2,2880]{3,2,0,1:T(2,128)(2,1)S(1)} reshape(bf16[256,2880]{1,0:T(8,128)(2,1)} %copy.25) | data formatting | bytes 2949120 | tf_op jit(solution)/shard_map/stack;reshape | solution.py:37
  13.9 4.4 %pad_maximum_fusion = bf16[128,2,2,2880]{3,2,0,1:T(2,128)(2,1)S(1)} fusion(bf16[128,1,2,2880]{3,2,0,1:T(2,128)(2,1)S(1)} %stack_reshape.7, bf16[128,1,2,2880]{3,2,0,1:T(2,128)(2,1)S(1)} %stack_reshape.6), kind=kLoop, calls=%fused_computation.9 | loop fusion | flops 1474560 | bytes 5898240 | tf_op jit(solution)/shard_map/stack | solution.py:37
  18.4 3.7 %copy.28 = bf16[128,2,2,2880]{3,2,1,0:T(2,128)(2,1)} copy(bf16[128,2,2,2880]{3,2,0,1:T(2,128)(2,1)S(1)} %pad_maximum_fusion) | data formatting | bytes 5898240 | tf_op jit(solution)/shard_map/stack | solution.py:37
  22.1 13.9 %all-to-all-start = ((bf16[128,2,2,2880]{3,2,1,0:T(2,128)(2,1)}), bf16[128,2,2,2880]{3,2,1,0:T(2,128)(2,1)S(1)}, u32[]{:S(2)}, u32[]{:S(2)}) async-start(bf16[128,2,2,2880]{3,2,1,0:T(2,128)(2,1)} %copy.28), calls=%async_computation | async-start | bytes 6029312 | tf_op jit(solution)/shard_map/all_to_all | solution.py:44
  37.3 68.5 %all-to-all-done = bf16[128,2,2,2880]{3,2,1,0:T(2,128)(2,1)S(1)} async-done(((bf16[128,2,2,2880]{3,2,1,0:T(2,128)(2,1)}), bf16[128,2,2,2880]{3,2,1,0:T(2,128)(2,1)S(1)}, u32[]{:S(2)}, u32[]{:S(2)}) %all-to-all-start) | async-done | bytes 2949152 | tf_op jit(solution)/shard_map/all_to_all | solution.py:44
  105.8 3.3 %fusion.31 = (bf16[128,1,2,2880]{3,2,1,0:T(2,128)(2,1)}, bf16[128,1,2,2880]{3,2,1,0:T(2,128)(2,1)}) fusion(bf16[128,2,2,2880]{3,2,1,0:T(2,128)(2,1)S(1)} %all-to-all-done), kind=kLoop, calls=%fused_computation.48 | loop fusion | bytes 5898240 | tf_op jit(solution)/shard_map/slice | solution.py:46
  109.1 3.5 %reshape_squeeze.7 = bf16[256,2880]{1,0:T(8,128)(2,1)S(1)} reshape(bf16[128,1,2,2880]{3,2,1,0:T(2,128)(2,1)} %get-tuple-element.3) | data formatting | bytes 2949120 | tf_op jit(solution)/shard_map/reshape;squeeze | solution.py:45
  112.6 3.5 %fusion.15 = f32[480,256]{1,0:T(8,128)} fusion(bf16[256,2880]{1,0:T(8,128)(2,1)S(1)} %reshape_squeeze.7, bf16[480,8640]{1,0:T(8,128)(2,1)} %bitcast.41), kind=kOutput, calls=%fused_computation.20 | convolution fusion | flops 707788800 | bytes 4792320 | tf_op jit(solution)/shard_map/dot_general | solution.py:11
  116.1 3.9 %fusion.12 = f32[480,256]{1,0:T(8,128)} fusion(bf16[256,2880]{1,0:T(8,128)(2,1)S(1)} %reshape_squeeze.7, bf16[480,8640]{1,0:T(8,128)(2,1)} %bitcast.42), kind=kOutput, calls=%fused_computation.19 | convolution fusion | flops 707788800 | bytes 4792320 | tf_op jit(solution)/shard_map/dot_general | solution.py:11
  120.1 3.5 %reshape_squeeze.6 = bf16[256,2880]{1,0:T(8,128)(2,1)S(1)} reshape(bf16[128,1,2,2880]{3,2,1,0:T(2,128)(2,1)} %get-tuple-element.2) | data formatting | bytes 2949120 | tf_op jit(solution)/shard_map/reshape;squeeze | solution.py:46
  123.6 1.6 copy.31
  125.2 2.9 %collective-permute-start.2 = (bf16[256,2880]{0,1:T(8,128)(2,1)}, bf16[256,2880]{0,1:T(8,128)(2,1)}, u32[]{:S(2)}, u32[]{:S(2)}) collective-permute-start(bf16[256,2880]{0,1:T(8,128)(2,1)} %copy.31), channel_id=1, source_target_pairs={{0,128},{128,0},{1,129},{129,1},{2,130},{130,2},{3,131},{131,3},{4... | collective-permute-start | bytes 4423688 | tf_op jit(solution)/shard_map/ppermute | solution.py:17
  128.1 3.8 %fusion.22 = (bf16[1,480,256]{2,1,0:T(8,128)(2,1)}, bf16[480,256]{1,0:T(8,128)(2,1)S(1)}, bf16[480,256]{1,0:T(8,128)(2,1)S(1)}) fusion(f32[480,256]{1,0:T(8,128)} %fusion.12, f32[480]{0:T(512)S(1)} %fusion.26, f32[480,256]{1,0:T(8,128)} %fusion.15, bf16[256,2880]{1,0:T(8,128)(2,1)S(1)} %reshape_squeeze.6, bf16[480,8640]{1,0:T(8,128)(2,1)} %bitcast.43), kind=kOutput, calls=%fused_computation.30 | convolution fusion | flops 710000640 | bytes 6023040 | tf_op jit(solution)/shard_map/dot_general | solution.py:11
  131.9 3.2 %fusion.5 = f32[256,2880]{0,1:T(8,128)S(1)} fusion(bf16[480,256]{1,0:T(8,128)(2,1)S(1)} %get-tuple-element.7, bf16[480,8640]{1,0:T(8,128)(2,1)} %bitcast.44), kind=kOutput, calls=%fused_computation.12 | convolution fusion | flops 707788800 | bytes 6021120 | tf_op jit(solution)/shard_map/dot_general | solution.py:11
  135.2 6.0 %fusion.1 = bf16[256,2880]{0,1:T(8,128)(2,1)} fusion(f32[256,2880]{0,1:T(8,128)S(1)} %fusion.5, bf16[480,256]{1,0:T(8,128)(2,1)S(1)} %get-tuple-element.8, bf16[480,8640]{1,0:T(8,128)(2,1)} %bitcast.45), kind=kOutput, calls=%fused_computation.5 | convolution fusion | flops 709263360 | bytes 7495680 | tf_op jit(solution)/shard_map/dot_general | solution.py:11
  141.2 2.5 %copy.29 = bf16[256,2880]{1,0:T(8,128)(2,1)} copy(bf16[256,2880]{0,1:T(8,128)(2,1)} %fusion.1) | data formatting | bytes 2949120 | tf_op jit(solution)/shard_map/convert_element_type | solution.py:74
  143.7 4.3 %reshape.96 = bf16[128,2,2880]{2,1,0:T(2,128)(2,1)} reshape(bf16[256,2880]{1,0:T(8,128)(2,1)} %copy.29) | data formatting | bytes 2949120 | tf_op jit(solution)/shard_map/reshape | solution.py:76
  148.0 8.6 %all-to-all-start.1 = ((bf16[128,2,2880]{2,1,0:T(2,128)(2,1)}), bf16[128,2,2880]{2,1,0:T(2,128)(2,1)}, u32[]{:S(2)}, u32[]{:S(2)}) async-start(bf16[128,2,2880]{2,1,0:T(2,128)(2,1)} %reshape.96), calls=%async_computation.1 | async-start | bytes 3014656 | tf_op jit(solution)/shard_map/all_to_all | solution.py:75
  160.8 2.2 collective-permute-start
  164.5 52.5 %collective-permute-done = bf16[3,240,256]{2,1,0:T(8,128)(2,1)S(1)} collective-permute-done((bf16[3,240,256]{2,1,0:T(8,128)(2,1)S(1)}, bf16[3,240,256]{2,1,0:T(8,128)(2,1)S(1)}, u32[]{:S(2)}, u32[]{:S(2)}) %collective-permute-start) | collective-permute-done | bytes 368672 | tf_op jit(solution)/shard_map/ppermute | solution.py:17
  217.0 2.0 fusion.2
  221.4 7.4 %concatenate.3 = bf16[240,8640]{1,0:T(8,128)(2,1)} concatenate(bf16[240,2880]{1,0:T(8,128)(2,1)} %get-tuple-element.5, bf16[240,2880]{1,0:T(8,128)(2,1)S(1)} %get-tuple-element.4, bf16[240,2880]{1,0:T(8,128)(2,1)S(1)} %fusion.2), dimensions={1} | concatenate | bytes 8294400 | tf_op jit(solution)/shard_map/concatenate | solution.py:88
  228.8 3.5 %reshape.97 = bf16[256,2880]{1,0:T(8,128)(2,1)S(1)} reshape(bf16[128,2,2880]{2,1,0:T(2,128)(2,1)} %all-to-all-done.1) | data formatting | bytes 2949120 | tf_op jit(solution)/shard_map/reshape | solution.py:82
  (42 shorter events, 18.4 us)
Async XLA Ops:
  0.6 5.0 %copy-start = (bf16[16,2880]{1,0:T(8,128)(2,1)S(1)}, bf16[16,2880]{1,0:T(8,128)(2,1)}, u32[]{:S(2)}) copy-start(bf16[16,2880]{1,0:T(8,128)(2,1)} %param.8) | copy-start | bytes 276484
  7.4 0.9 copy-start.3
  22.1 14.0 %copy-start.4 = (s32[128]{0:T(128)S(1)}, s32[128]{0:T(128)}, u32[]{:S(2)}) copy-start(s32[128]{0:T(128)} %param.12) | copy-start | bytes 1540
  22.1 83.8 %all-to-all-start = ((bf16[128,2,2,2880]{3,2,1,0:T(2,128)(2,1)}), bf16[128,2,2,2880]{3,2,1,0:T(2,128)(2,1)S(1)}, u32[]{:S(2)}, u32[]{:S(2)}) async-start(bf16[128,2,2,2880]{3,2,1,0:T(2,128)(2,1)} %copy.28), calls=%async_computation | async-start | bytes 6029312 | tf_op jit(solution)/shard_map/all_to_all | solution.py:44
  125.2 91.8 %collective-permute-start.2 = (bf16[256,2880]{0,1:T(8,128)(2,1)}, bf16[256,2880]{0,1:T(8,128)(2,1)}, u32[]{:S(2)}, u32[]{:S(2)}) collective-permute-start(bf16[256,2880]{0,1:T(8,128)(2,1)} %copy.31), channel_id=1, source_target_pairs={{0,128},{128,0},{1,129},{129,1},{2,130},{130,2},{3,131},{131,3},{4... | collective-permute-start | bytes 4423688 | tf_op jit(solution)/shard_map/ppermute | solution.py:17
  131.9 3.2 %copy-start.2 = (bf16[480,256]{1,0:T(8,128)(2,1)}, bf16[480,256]{1,0:T(8,128)(2,1)S(1)}, u32[]{:S(2)}) copy-start(bf16[480,256]{1,0:T(8,128)(2,1)S(1)} %get-tuple-element.8) | copy-start | bytes 737284
  148.0 80.8 %all-to-all-start.1 = ((bf16[128,2,2880]{2,1,0:T(2,128)(2,1)}), bf16[128,2,2880]{2,1,0:T(2,128)(2,1)}, u32[]{:S(2)}, u32[]{:S(2)}) async-start(bf16[128,2,2880]{2,1,0:T(2,128)(2,1)} %reshape.96), calls=%async_computation.1 | async-start | bytes 3014656 | tf_op jit(solution)/shard_map/all_to_all | solution.py:75
  158.1 60.9 %collective-permute-start.1 = (bf16[256,2880]{0,1:T(8,128)(2,1)}, bf16[256,2880]{0,1:T(8,128)(2,1)S(1)}, u32[]{:S(2)}, u32[]{:S(2)}) collective-permute-start(bf16[256,2880]{0,1:T(8,128)(2,1)} %copy.30), channel_id=1, source_target_pairs={{0,128},{128,0},{1,129},{129,1},{2,130},{130,2},{3,131},{131,3},{4... | collective-permute-start | bytes 4423688 | tf_op jit(solution)/shard_map/ppermute | solution.py:17
  160.8 56.2 %collective-permute-start = (bf16[3,240,256]{2,1,0:T(8,128)(2,1)S(1)}, bf16[3,240,256]{2,1,0:T(8,128)(2,1)S(1)}, u32[]{:S(2)}, u32[]{:S(2)}) collective-permute-start(bf16[3,240,256]{2,1,0:T(8,128)(2,1)S(1)} %constant_dynamic-slice_fusion.1), channel_id=1, source_target_pairs={{0,128},{128,0},{1,129},{129,1},{2,130},{130,2},{3,131},{131,3},{4... | collective-permute-start | bytes 1105928 | tf_op jit(solution)/shard_map/ppermute | solution.py:17
  228.8 4.5 %copy-start.1 = (bf16[16,2880]{1,0:T(8,128)(2,1)S(1)}, bf16[16,2880]{1,0:T(8,128)(2,1)}, u32[]{:S(2)}) copy-start(bf16[16,2880]{1,0:T(8,128)(2,1)} %param.8) | copy-start | bytes 276484

commit v2 on v1

v2 whole, which is shorter than its diff:
```python
import jax
import jax.numpy as jnp
from jax import lax
from jax.experimental import pallas as pl
from jax.experimental.pallas import tpu as pltpu
from jax.sharding import Mesh, PartitionSpec as P

F32 = jnp.float32
BF16 = jnp.bfloat16
D = 2880
WIDE = 2944
EDGE = 2816
LAST = D - EDGE
TOKENS = 16
TOPK = 4
PLANES = 8
PEERS = 16
GROUP = 5
SLOTS = 2 * GROUP
PACKED = 24
ROWS = 256
GATHERED = PLANES * 16
UNITS = 480
HALF = 240
STEP = 512
PLANE = ("x", "y", "c")
ALL = ("dp", "z", "x", "y", "c")

VMEM = pl.BlockSpec(memory_space=pltpu.VMEM)
SMEM = pl.BlockSpec(memory_space=pltpu.SMEM)
WAITED = pl.BlockSpec(memory_space=pl.ANY)


def dot(left, right, left_dim, right_dim):
    return lax.dot_general(
        left, right, (((left_dim,), (right_dim,)), ((), ())), preferred_element_type=F32
    )


def chunks(total):
    return [(at, min(STEP, total - at)) for at in range(0, total, STEP)]


def iota(shape, dim):
    return lax.broadcasted_iota(jnp.int32, shape, dim)


def call(kernel, out_shape, in_specs, flops, moved, scratch=(), mib=24):
    outs = jax.tree.map(lambda _: VMEM, out_shape)
    return pl.pallas_call(
        kernel,
        out_shape=out_shape,
        in_specs=in_specs,
        out_specs=outs,
        scratch_shapes=list(scratch),
        compiler_params=pltpu.CompilerParams(vmem_limit_bytes=mib << 20),
        cost_estimate=pl.CostEstimate(flops=flops, bytes_accessed=moved, transcendentals=0),
    )


def shape(dims, kind=BF16):
    return jax.ShapeDtypeStruct(dims, kind)


def pack_kernel(plane_ref, token_ref, grad_ref, id_ref, prob_ref, *out_refs):
    grid = (TOKENS, ROWS)
    row = iota(grid, 1)
    hop = (row * 2731) >> 16
    slot = row - PACKED * hop
    is_grad = slot >= SLOTS
    slot = jnp.where(is_grad, slot - SLOTS, slot)
    expert = GROUP * ((plane_ref[0] + hop) & (PLANES - 1)) + (slot >> 1)
    picked, weight = pick_tokens(id_ref, prob_ref, expert, slot)
    scale = jnp.sum(picked * weight, axis=0, keepdims=True)
    scale = jnp.where(is_grad[:1], scale, 0.0)
    scale = jnp.broadcast_to(scale, (TOKENS, ROWS)).T[:, :1]
    want_grad = jnp.where(is_grad, 1.0, 0.0).T[:, :1] > 0.5
    picked = picked.T.astype(BF16)
    for at, size in chunks(WIDE):
        end = min(at + size, D)
        value = jnp.where(
            want_grad,
            scale * dot(picked, grad_ref[:, at:end], 1, 0),
            dot(picked, token_ref[:, at:end], 1, 0),
        )
        if end < at + size:
            value = jnp.concatenate([value, jnp.zeros((ROWS, at + size - end), F32)], axis=1)
        for k, out_ref in enumerate(out_refs):
            out_ref[:, at : at + size] = value[PACKED * k : PACKED * (k + 1)].astype(BF16)


def pick_tokens(id_ref, prob_ref, expert, slot):
    has = jnp.zeros(expert.shape, F32)
    weight = jnp.zeros(expert.shape, F32)
    ids = id_ref[...]
    for k in range(TOPK):
        match = ids[:, k : k + 1] == expert
        has = jnp.where(match, 1.0, has)
        if prob_ref is not None:
            weight = jnp.where(match, prob_ref[:, k : k + 1], weight)
    square = (TOKENS, TOKENS)
    earlier = (iota(square, 1) < iota(square, 0)).astype(F32).astype(BF16)
    rank = dot(earlier, has.astype(BF16), 1, 0).astype(jnp.int32)
    wanted = (has > 0.5) & (rank == (slot & 1)) & (slot < SLOTS)
    return jnp.where(wanted, 1.0, 0.0), weight


def local_slot(expert_ref, plane_ref, row):
    local = jnp.zeros(row.shape, jnp.int32)
    for peer in range(PEERS):
        named = expert_ref[plane_ref[0] * PEERS + peer] - GROUP * plane_ref[0]
        local = jnp.where((row >> 4) == peer, named, local)
    return 2 * local + (row & 1)


def pick_kernel(expert_ref, plane_ref, *refs):
    blocks, (row_ref, grad_ref) = refs[:PLANES], refs[PLANES:]
    grid = (ROWS, ROWS)
    row, column = iota(grid, 0), iota(grid, 1)
    source = PACKED * ((row >> 1) & (PLANES - 1)) + local_slot(expert_ref, plane_ref, row)
    column = column[:, : PLANES * PACKED]
    source = source[:, : PLANES * PACKED]
    pick_row = (column == source).astype(F32).astype(BF16)
    pick_grad = (column == source + SLOTS).astype(F32).astype(BF16)
    for at, size in chunks(WIDE):
        block = jnp.concatenate(
            [ref[:, at : at + size].astype(F32) for ref in blocks], axis=0
        ).astype(BF16)
        row_ref[:, at : at + size] = dot(pick_row, block, 1, 0).astype(BF16)
        keep = min(at + size, D) - at
        grad_ref[:, at : at + keep] = dot(pick_grad, block, 1, 0)[:, :keep].astype(BF16)


def shifted(rows):
    return pltpu.roll(rows.astype(F32), LAST, 1).astype(BF16)


def unit_kernel(
    limit_ref, replica_ref, row_ref, grad_ref, weight_ref, own_ref, other_ref, part_ref, shift_ref
):
    shift_ref[...] = shifted(row_ref[...])
    gate = dot(weight_ref[:, :WIDE], row_ref[...], 1, 1)
    up = dot(weight_ref[:, EDGE : 2 * D], shift_ref[...], 1, 1)
    back = dot(weight_ref[:, 2 * D :], grad_ref[...], 1, 1)
    mask = jnp.where(iota(gate.shape, 0) < limit_ref[0], 1.0, 0.0)
    sigma = jax.nn.sigmoid(gate)
    active = gate * sigma * mask
    hidden = (active * up).astype(BF16)
    grad_gate = (back * up * (sigma * (1.0 + gate * (1.0 - sigma))) * mask).astype(BF16)
    grad_up = (back * active).astype(BF16)
    for half in range(2):
        for target, mine in ((own_ref, half), (other_ref, 1 - half)):

            @pl.when(replica_ref[0] == mine)
            def _(target=target, at=half * HALF):
                target[0] = grad_gate[at : at + HALF]
                target[1] = grad_up[at : at + HALF]
                target[2] = hidden[at : at + HALF]

    gate_rows = grad_gate.astype(F32).T.astype(BF16)
    up_rows = grad_up.astype(F32).T.astype(BF16)
    for at, size in chunks(WIDE):
        end = at + size
        value = dot(gate_rows, weight_ref[:, at:end], 1, 0)
        wide = dot(up_rows, weight_ref[:, EDGE + at : min(EDGE + end + 128, 2 * D)], 1, 0)
        value = value + pltpu.roll(wide, wide.shape[1] - LAST, 1)[:, :size]
        keep = min(end, D) - at
        part_ref[:, at : at + keep] = value[:, :keep].astype(BF16)


def weight_kernel(
    own_ref, other_ref, row_ref, far_row_ref, grad_ref, far_grad_ref, out_ref, shift_ref, far_shift_ref
):
    shift_ref[...] = shifted(row_ref[...])
    far_shift_ref[...] = shifted(far_row_ref[...])

    def term(which, near, far, at, end):
        return dot(own_ref[which], near[:, at:end], 1, 0) + dot(
            other_ref[which], far[:, at:end], 1, 0
        )

    for at, size in chunks(EDGE):
        value = term(0, row_ref, far_row_ref, at, at + size)
        out_ref[0, :, at : at + size] = value.astype(BF16)
    value = term(0, row_ref, far_row_ref, EDGE, WIDE) + term(1, shift_ref, far_shift_ref, 0, 128)
    out_ref[0, :, EDGE:WIDE] = value.astype(BF16)
    for at, size in chunks(WIDE - 128):
        value = term(1, shift_ref, far_shift_ref, 128 + at, 128 + at + size)
        out_ref[0, :, WIDE + at : WIDE + at + size] = value.astype(BF16)
    for at, size in chunks(D):
        value = term(2, grad_ref, far_grad_ref, at, at + size)
        out_ref[0, :, 2 * D + at : 2 * D + at + size] = value.astype(BF16)


def gather_kernel(expert_ref, plane_ref, part_ref, _, __, out_ref):
    grid = (GATHERED, ROWS)
    row, column = iota(grid, 0), iota(grid, 1)
    same_hop = (row >> 4) == ((column >> 1) & (PLANES - 1))
    same_slot = (row & 15) == local_slot(expert_ref, plane_ref, column)
    picked = (same_hop & same_slot).astype(F32).astype(BF16)
    for at, size in chunks(D):
        value = dot(picked, part_ref[:, at : at + size], 1, 0).astype(BF16)
        for k in range(PLANES):
            source = (plane_ref[0] + PLANES - k) & (PLANES - 1)
            out_ref[source, :, at : at + size] = value[TOKENS * k : TOKENS * (k + 1)]


def sum_kernel(part_ref, id_ref, _, out_ref):
    row = iota((TOKENS, GATHERED), 1)
    slot = row & 15
    picked, _ = pick_tokens(id_ref, None, GROUP * (row >> 4) + (slot >> 1), slot)
    picked = picked.astype(BF16)
    for at, size in chunks(D):
        value = dot(picked, part_ref[:, at : at + size], 1, 0)
        out_ref[:, at : at + size] = value.astype(BF16)


def along_z(value, by):
    return lax.ppermute(value, "z", [(i, (i + by) % PLANES) for i in range(PLANES)])


def swap_dp(value):
    return lax.ppermute(value, "dp", [(0, 1), (1, 0)])


def swap_rows(rows):
    blocks = rows.reshape(PEERS, ROWS // PEERS, rows.shape[1])
    return swap_dp(blocks).reshape(rows.shape)


def in_plane(rows):
    blocks = rows.reshape(PEERS, ROWS // PEERS, rows.shape[1])
    blocks = lax.all_to_all(blocks, PLANE, split_axis=0, concat_axis=0, tiled=True)
    return blocks.reshape(rows.shape)


FAR_FIRST = (4, 3, 5, 2, 6, 1, 7)


def to_planes(blocks):
    sent = {by: along_z(blocks[by], by) for by in FAR_FIRST}
    return [blocks[0]] + [sent[by] for by in range(1, PLANES)]


def shards(tokens, grad_out, route_ids, route_prob, device_expert, unit_count, expert_weights):
    plane = lax.axis_index("z").astype(jnp.int32)
    replica = lax.axis_index("dp").astype(jnp.int32).reshape(1)
    limit = lax.dynamic_slice_in_dim(unit_count, plane * PEERS + lax.axis_index(PLANE), 1)
    slot_weights = expert_weights[0]

    plane = plane.reshape(1)
    row_flops = 2 * ROWS * D
    packed = call(
        pack_kernel,
        [shape((PACKED, WIDE))] * PLANES,
        [SMEM] + [VMEM] * 4,
        row_flops * TOKENS,
        1_400_000,
    )(plane, tokens, grad_out, route_ids, route_prob)
    blocks = to_planes(packed)
    sent_rows, sent_grads = call(
        pick_kernel,
        (shape((ROWS, WIDE)), shape((ROWS, D))),
        [SMEM, SMEM] + [VMEM] * PLANES,
        2 * row_flops * PLANES * PACKED,
        4_200_000,
    )(device_expert, plane, *blocks)
    token_rows = in_plane(sent_rows)
    far_token_rows = swap_rows(token_rows)
    grad_rows = in_plane(sent_grads)
    far_grad_rows = swap_rows(grad_rows)

    own, other, part = call(
        unit_kernel,
        (shape((3, HALF, ROWS)), shape((3, HALF, ROWS)), shape((ROWS, D))),
        [SMEM, SMEM] + [VMEM] * 3,
        5 * row_flops * UNITS,
        14_000_000,
        [pltpu.VMEM((ROWS, WIDE), BF16)],
        40,
    )(limit, replica, token_rows, grad_rows, slot_weights)
    other = swap_dp(other)

    returned = in_plane(part)
    token_parts = call(
        gather_kernel,
        shape((PLANES, TOKENS, D)),
        [SMEM, SMEM, VMEM, WAITED, WAITED],
        row_flops * GATHERED,
        2_400_000,
    )(device_expert, plane, returned, far_token_rows, other)
    home = lax.all_to_all(token_parts, "z", split_axis=0, concat_axis=0, tiled=True)
    grad_weights = call(
        weight_kernel,
        shape((1, HALF, 3 * D)),
        [VMEM] * 6,
        3 * row_flops * UNITS,
        12_000_000,
        [pltpu.VMEM((ROWS, WIDE), BF16)] * 2,
        40,
    )(own, other, token_rows, far_token_rows, grad_rows, far_grad_rows)
    grad_tokens = call(
        sum_kernel, shape((TOKENS, D)), [VMEM, VMEM, WAITED], row_flops, 900_000
    )(home.reshape(GATHERED, D), route_ids, far_grad_rows)
    return grad_tokens, grad_weights


def solution(mesh):
    fine = Mesh(mesh.devices.reshape(2, PLANES, 4, 2, 2), ALL)
    slots = ("z",) + PLANE
    in_specs = (P(ALL), P(ALL), P(ALL), P(ALL), P(), P(), P(slots))
    out_specs = (P(ALL), P(slots, "dp"))
    return jax.shard_map(shards, mesh=fine, in_specs=in_specs, out_specs=out_specs, check_vma=False)
```

time: 235 us -> 195 us (0.83)
  local copies, waits for them, and re-layouts: 47 us -> 12.9 us
  waiting for transfers between devices: 121 us -> 91.3 us
  matrix products: 27.3 us -> 0 us
  blocking collectives: 0 us -> 24.7 us
  Pallas kernels: 0 us -> 19.4 us
  starting transfers between devices: 29 us -> 43.8 us
  other arithmetic: 8.08 us -> 0 us
    all_to_all x2 -> x3, waiting for transfers between devices: 68.6 us -> 16.3 us  [the longest x2 16.2 us: in_plane(): lax.all_to_all(blocks, PLANE, split_axis=0, concat_axis=0, tiled=True)]
    dot_general x12 -> x0, matrix products: 27.3 us -> none  [dot(): lax.dot_general(left, right, (((left_dim,), (right_dim,)), ((), ())), pre...]
    all_to_all x0 -> x1, blocking collectives: none -> 24.7 us  [in_plane(): lax.all_to_all(blocks, PLANE, split_axis=0, concat_axis=0, tiled=True)]
    ppermute x0 -> x7, starting transfers between devices: none -> 19.8 us  [along_z(): lax.ppermute(value, 'z', [(i, (i + by) % PLANES) for i in range(PLANES)])]
    pallas_call x0 -> x6, Pallas kernels: none -> 19.4 us  [the longest x1 7.08 us: shards(): call(unit_kernel, (shape((3, HALF, ROWS)), shape((3, HALF, ROWS)), shape(...]
    another operation x7 -> x0, local copies, waits for them, and re-layouts: 17.8 us -> none  [the longest x3 7.65 us: shards(): jnp.stack([sent_rows.reshape(devices, capacity, width), sent_grads.reshap...]
    ppermute x0 -> x7, waiting for transfers between devices: none -> 16.2 us  [along_z(): lax.ppermute(value, 'z', [(i, (i + by) % PLANES) for i in range(PLANES)])]
    unnamed x12 -> x30, local copies, waits for them, and re-layouts: 1.84 us -> 12.4 us
  transfers between devices with their start and end apart: 5 -> 13, of which waited for: 2 -> 8; matrix products, arithmetic and copies ran while one was open for 16% -> 0% of each run, Pallas kernels for 0% -> 7%
where the time goes in v2:
time: 195 us; the launch traced here: 193 us
  waiting for transfers between devices  91.3 us (47%)
  starting transfers between devices  43.8 us (22%)
  blocking collectives  24.7 us (13%)
  Pallas kernels  19.4 us (10%)
  local copies, waits for them, and re-layouts  12.9 us (7%)
    ppermute x3, waiting for transfers between devices, swap_dp(): return lax.ppermute(value, 'dp', [(0, 1), (1, 0)])  58.9 us
    all_to_all x1, blocking collectives, in_plane(): lax.all_to_all(blocks, PLANE, split_axis=0, concat_axis=0, tiled=True)  24.7 us
    ppermute x7, starting transfers between devices, along_z(): lax.ppermute(value, 'z', [(i, (i + by) % PLANES) for i in range(PLANES)])  19.8 us
    all_to_all x2, waiting for transfers between devices, in_plane(): lax.all_to_all(blocks, PLANE, split_axis=0, concat_axis=0, tiled=True)  16.2 us
    ppermute x7, waiting for transfers between devices, along_z(): lax.ppermute(value, 'z', [(i, (i + by) % PLANES) for i in range(PLANES)])  16.2 us
    unnamed x30, local copies, waits for them, and re-layouts  12.4 us
    all_to_all x2, starting transfers between devices, in_plane(): lax.all_to_all(blocks, PLANE, split_axis=0, concat_axis=0, tiled=True)  12.3 us
    pallas_call x1, Pallas kernels, shards(): call(unit_kernel, (shape((3, HALF, ROWS)), shape((3, HALF, ROWS)), shape(...  7.08 us
  transfers between devices with their start and end apart: 13, of which 8 were waited for; matrix products, arithmetic and copies ran while one was open for 0% of the time, Pallas kernels for 7%

profile of v2, /device:TPU:2, one launch (start us, length us, event | category | flops | bytes accessed | tf_op | source)
XLA Modules:
  0.0 192.9 jit_solution(10814815945184528410)
XLA Ops:
  5.2 2.0 %collective-permute-start = (bf16[24,2944]{1,0:T(8,128)(2,1)S(1)}, bf16[24,2944]{1,0:T(8,128)(2,1)S(1)}, u32[]{:S(2)}, u32[]{:S(2)}) collective-permute-start(bf16[24,2944]{1,0:T(8,128)(2,1)S(1)} %get-tuple-element.16), channel_id=1, source_target_pairs={{0,16},{16,32},{32,48},{48,64},{64,80},{80,96},{96,112},{112,0},{1... | collective-permute-start | bytes 423944 | tf_op jit(solution)/shard_map/ppermute | solution.py:219
  7.2 3.3 %collective-permute-start.1 = (bf16[24,2944]{1,0:T(8,128)(2,1)S(1)}, bf16[24,2944]{1,0:T(8,128)(2,1)S(1)}, u32[]{:S(2)}, u32[]{:S(2)}) collective-permute-start(bf16[24,2944]{1,0:T(8,128)(2,1)S(1)} %get-tuple-element.17), channel_id=1, source_target_pairs={{0,32},{16,48},{32,64},{48,80},{64,96},{80,112},{96,0},{112,16},{1... | collective-permute-start | bytes 423944 | tf_op jit(solution)/shard_map/ppermute | solution.py:219
  10.4 4.0 %collective-permute-start.2 = (bf16[24,2944]{1,0:T(8,128)(2,1)S(1)}, bf16[24,2944]{1,0:T(8,128)(2,1)S(1)}, u32[]{:S(2)}, u32[]{:S(2)}) collective-permute-start(bf16[24,2944]{1,0:T(8,128)(2,1)S(1)} %get-tuple-element.18), channel_id=1, source_target_pairs={{0,48},{16,64},{32,80},{48,96},{64,112},{80,0},{96,16},{112,32},{1... | collective-permute-start | bytes 423944 | tf_op jit(solution)/shard_map/ppermute | solution.py:219
  15.0 4.9 %collective-permute-start.4 = (bf16[24,2944]{1,0:T(8,128)(2,1)S(1)}, bf16[24,2944]{1,0:T(8,128)(2,1)S(1)}, u32[]{:S(2)}, u32[]{:S(2)}) collective-permute-start(bf16[24,2944]{1,0:T(8,128)(2,1)S(1)} %get-tuple-element.20), channel_id=1, source_target_pairs={{0,80},{16,96},{32,112},{48,0},{64,16},{80,32},{96,48},{112,64},{1... | collective-permute-start | bytes 423944 | tf_op jit(solution)/shard_map/ppermute | solution.py:219
  20.0 2.7 %collective-permute-start.5 = (bf16[24,2944]{1,0:T(8,128)(2,1)S(1)}, bf16[24,2944]{1,0:T(8,128)(2,1)S(1)}, u32[]{:S(2)}, u32[]{:S(2)}) collective-permute-start(bf16[24,2944]{1,0:T(8,128)(2,1)S(1)} %get-tuple-element.21), channel_id=1, source_target_pairs={{0,96},{16,112},{32,0},{48,16},{64,32},{80,48},{96,64},{112,80},{1... | collective-permute-start | bytes 423944 | tf_op jit(solution)/shard_map/ppermute | solution.py:219
  22.6 2.1 %collective-permute-done.1.refs_2_ = bf16[24,2944]{1,0:T(8,128)(2,1)S(1)} collective-permute-done((bf16[24,2944]{1,0:T(8,128)(2,1)S(1)}, bf16[24,2944]{1,0:T(8,128)(2,1)S(1)}, u32[]{:S(2)}, u32[]{:S(2)}) %collective-permute-start.1) | collective-permute-done | bytes 141344 | tf_op jit(solution)/shard_map/ppermute | solution.py:219
  24.8 2.4 %collective-permute-start.6 = (bf16[24,2944]{1,0:T(8,128)(2,1)S(1)}, bf16[24,2944]{1,0:T(8,128)(2,1)S(1)}, u32[]{:S(2)}, u32[]{:S(2)}) collective-permute-start(bf16[24,2944]{1,0:T(8,128)(2,1)S(1)} %get-tuple-element.22), channel_id=1, source_target_pairs={{0,112},{16,0},{32,16},{48,32},{64,48},{80,64},{96,80},{112,96},{1... | collective-permute-start | bytes 423944 | tf_op jit(solution)/shard_map/ppermute | solution.py:219
  27.1 6.5 %collective-permute-done.2.refs_3_ = bf16[24,2944]{1,0:T(8,128)(2,1)S(1)} collective-permute-done((bf16[24,2944]{1,0:T(8,128)(2,1)S(1)}, bf16[24,2944]{1,0:T(8,128)(2,1)S(1)}, u32[]{:S(2)}, u32[]{:S(2)}) %collective-permute-start.2) | collective-permute-done | bytes 141344 | tf_op jit(solution)/shard_map/ppermute | solution.py:219
  33.6 3.3 %collective-permute-done.4.refs_5_ = bf16[24,2944]{1,0:T(8,128)(2,1)S(1)} collective-permute-done((bf16[24,2944]{1,0:T(8,128)(2,1)S(1)}, bf16[24,2944]{1,0:T(8,128)(2,1)S(1)}, u32[]{:S(2)}, u32[]{:S(2)}) %collective-permute-start.4) | collective-permute-done | bytes 141344 | tf_op jit(solution)/shard_map/ppermute | solution.py:219
  36.9 3.0 %collective-permute-done.5.refs_6_ = bf16[24,2944]{1,0:T(8,128)(2,1)S(1)} collective-permute-done((bf16[24,2944]{1,0:T(8,128)(2,1)S(1)}, bf16[24,2944]{1,0:T(8,128)(2,1)S(1)}, u32[]{:S(2)}, u32[]{:S(2)}) %collective-permute-start.5) | collective-permute-done | bytes 141344 | tf_op jit(solution)/shard_map/ppermute | solution.py:219
  41.8 1.7 shard_map.87
  43.5 24.7 %all_to_all.20 = bf16[16,16,2944]{2,1,0:T(8,128)(2,1)S(1)} all-to-all(bf16[16,16,2944]{2,1,0:T(8,128)(2,1)S(1)} %bitcast.19), channel_id=1, replica_groups=mesh['dp'=2,'z'=8,'x'=4,'y'=2,'c'=2] {'x','y','c'}, dimensions={0} | all-to-all | bytes 3014656 | tf_op jit(solution)/shard_map/all_to_all | solution.py:233
  68.2 6.1 %all-to-all-start.1 = ((bf16[16,16,2880]{2,1,0:T(8,128)(2,1)}), bf16[16,16,2880]{2,1,0:T(8,128)(2,1)S(1)}, u32[]{:S(2)}, u32[]{:S(2)}) async-start(bf16[16,16,2880]{2,1,0:T(8,128)(2,1)} %bitcast.17), calls=%async_computation.1 | async-start | bytes 3014656 | tf_op jit(solution)/shard_map/all_to_all | solution.py:233
  74.9 2.9 %collective-permute-start.7 = (bf16[16,16,2944]{2,1,0:T(8,128)(2,1)S(1)}, bf16[16,16,2944]{2,1,0:T(8,128)(2,1)}, u32[]{:S(2)}, u32[]{:S(2)}) collective-permute-start(bf16[16,16,2944]{2,1,0:T(8,128)(2,1)S(1)} %all_to_all.20), channel_id=1, source_target_pairs={{0,128},{128,0},{1,129},{129,1},{2,130},{130,2},{3,131},{131,3},{4... | collective-permute-start | bytes 4521992 | tf_op jit(solution)/shard_map/ppermute | solution.py:223
  77.8 16.2 %all-to-all-done.1 = bf16[16,16,2880]{2,1,0:T(8,128)(2,1)S(1)} async-done(((bf16[16,16,2880]{2,1,0:T(8,128)(2,1)}), bf16[16,16,2880]{2,1,0:T(8,128)(2,1)S(1)}, u32[]{:S(2)}, u32[]{:S(2)}) %all-to-all-start.1) | async-done | bytes 1474592 | tf_op jit(solution)/shard_map/all_to_all | solution.py:233
  94.0 3.9 %copy-done.11 = bf16[1,480,8640]{2,1,0:T(8,128)(2,1)S(1)} copy-done((bf16[1,480,8640]{2,1,0:T(8,128)(2,1)S(1)}, bf16[1,480,8640]{2,1,0:T(8,128)(2,1)}, u32[]{:S(2)}) %copy-start.11) | copy-done | bytes 8294424
  97.9 7.1 %shard_map.88 = (bf16[3,240,256]{2,1,0:T(8,128)(2,1)S(1)}, bf16[3,240,256]{2,1,0:T(8,128)(2,1)S(1)}, bf16[256,2880]{1,0:T(8,128)(2,1)S(1)}) custom-call(s32[1]{0:T(128)} %dynamic_slice.3.limit_ref, s32[1]{0:T(128)} %bitcast.1.replica_ref, bf16[256,2944]{1,0:T(8,128)(2,1)S(1)} %bitcast.13, bf16[256,2880]{1,0:T(8,128)(2,1)S(1)} %bitcast.15, ...), custom_call_target="tpu_custom_call" | custom-call | flops 3538944000 | bytes 14000000 | tf_op jit(solution)/shard_map/pallas_call | solution.py:273
  107.7 6.2 %all-to-all-start.2 = ((bf16[16,16,2880]{2,1,0:T(8,128)(2,1)}), bf16[16,16,2880]{2,1,0:T(8,128)(2,1)S(1)}, u32[]{:S(2)}, u32[]{:S(2)}) async-start(bf16[16,16,2880]{2,1,0:T(8,128)(2,1)} %bitcast.18), calls=%async_computation.2 | async-start | bytes 3014656 | tf_op jit(solution)/shard_map/all_to_all | solution.py:233
  113.9 2.9 %collective-permute-start.8 = (bf16[3,240,256]{2,1,0:T(8,128)(2,1)}, bf16[3,240,256]{2,1,0:T(8,128)(2,1)S(1)}, u32[]{:S(2)}, u32[]{:S(2)}) collective-permute-start(bf16[3,240,256]{2,1,0:T(8,128)(2,1)} %copy-done.12), channel_id=1, source_target_pairs={{0,128},{128,0},{1,129},{129,1},{2,130},{130,2},{3,131},{131,3},{4... | collective-permute-start | bytes 1105928 | tf_op jit(solution)/shard_map/ppermute | solution.py:223
  117.4 34.0 %collective-permute-done.8.__.other_ref = bf16[3,240,256]{2,1,0:T(8,128)(2,1)S(1)} collective-permute-done((bf16[3,240,256]{2,1,0:T(8,128)(2,1)}, bf16[3,240,256]{2,1,0:T(8,128)(2,1)S(1)}, u32[]{:S(2)}, u32[]{:S(2)}) %collective-permute-start.8) | collective-permute-done | bytes 368672 | tf_op jit(solution)/shard_map/ppermute | solution.py:223
  153.2 5.2 %all-to-all-start.3 = ((bf16[8,16,2880]{2,1,0:T(8,128)(2,1)}), bf16[8,16,2880]{2,1,0:T(8,128)(2,1)}, u32[]{:S(2)}, u32[]{:S(2)}) async-start(bf16[8,16,2880]{2,1,0:T(8,128)(2,1)} %copy-done.2), calls=%async_computation.3 | async-start | bytes 1507328 | tf_op jit(solution)/shard_map/all_to_all | solution.py:292
  158.4 24.9 %collective-permute-done.9 = bf16[16,16,2880]{2,1,0:T(8,128)(2,1)} collective-permute-done((bf16[16,16,2880]{2,1,0:T(8,128)(2,1)}, bf16[16,16,2880]{2,1,0:T(8,128)(2,1)}, u32[]{:S(2)}, u32[]{:S(2)}) %collective-permute-start.9) | collective-permute-done | bytes 1474592 | tf_op jit(solution)/shard_map/ppermute | solution.py:223
  184.3 6.4 %shard_map.91 = bf16[1,240,8640]{2,1,0:T(8,128)(2,1)} custom-call(bf16[3,240,256]{2,1,0:T(8,128)(2,1)S(1)} %copy-done.6, bf16[3,240,256]{2,1,0:T(8,128)(2,1)S(1)} %collective-permute-done.8.__.other_ref, bf16[256,2944]{1,0:T(8,128)(2,1)S(1)} %bitcast.14, bf16[256,2944]{1,0:T(8,128)(2,1)} %bitcast.9._.far_row_ref, bf16[256,2880]{1,0:T(8,128)(2,1)S(1)} %bitcast.16, ...), custom_call_target="tpu_custom_call" | custom-call | flops 2123366400 | bytes 12000000 | tf_op jit(solution)/shard_map/pallas_call | solution.py:293
  190.7 2.2 %shard_map.90 = bf16[16,2880]{1,0:T(8,128)(2,1)} custom-call(bf16[128,2880]{1,0:T(8,128)(2,1)} %bitcast.10.part_ref, s32[16,4]{1,0:T(8,128)S(1)} %copy.9.id_ref, bf16[256,2880]{1,0:T(8,128)(2,1)} %bitcast.11._.far_grad_ref), custom_call_target="tpu_custom_call" | custom-call | flops 1474560 | bytes 900000 | tf_op jit(solution)/shard_map/pallas_call | solution.py:302
  (40 shorter events, 13.6 us)
Async XLA Ops:
  2.2 0.9 copy-start.7
  3.0 0.9 copy-start.8
  5.2 14.8 %collective-permute-start = (bf16[24,2944]{1,0:T(8,128)(2,1)S(1)}, bf16[24,2944]{1,0:T(8,128)(2,1)S(1)}, u32[]{:S(2)}, u32[]{:S(2)}) collective-permute-start(bf16[24,2944]{1,0:T(8,128)(2,1)S(1)} %get-tuple-element.16), channel_id=1, source_target_pairs={{0,16},{16,32},{32,48},{48,64},{64,80},{80,96},{96,112},{112,0},{1... | collective-permute-start | bytes 423944 | tf_op jit(solution)/shard_map/ppermute | solution.py:219
  7.2 17.6 %collective-permute-start.1 = (bf16[24,2944]{1,0:T(8,128)(2,1)S(1)}, bf16[24,2944]{1,0:T(8,128)(2,1)S(1)}, u32[]{:S(2)}, u32[]{:S(2)}) collective-permute-start(bf16[24,2944]{1,0:T(8,128)(2,1)S(1)} %get-tuple-element.17), channel_id=1, source_target_pairs={{0,32},{16,48},{32,64},{48,80},{64,96},{80,112},{96,0},{112,16},{1... | collective-permute-start | bytes 423944 | tf_op jit(solution)/shard_map/ppermute | solution.py:219
  10.4 23.2 %collective-permute-start.2 = (bf16[24,2944]{1,0:T(8,128)(2,1)S(1)}, bf16[24,2944]{1,0:T(8,128)(2,1)S(1)}, u32[]{:S(2)}, u32[]{:S(2)}) collective-permute-start(bf16[24,2944]{1,0:T(8,128)(2,1)S(1)} %get-tuple-element.18), channel_id=1, source_target_pairs={{0,48},{16,64},{32,80},{48,96},{64,112},{80,0},{96,16},{112,32},{1... | collective-permute-start | bytes 423944 | tf_op jit(solution)/shard_map/ppermute | solution.py:219
  14.5 19.2 %collective-permute-start.3 = (bf16[24,2944]{1,0:T(8,128)(2,1)S(1)}, bf16[24,2944]{1,0:T(8,128)(2,1)S(1)}, u32[]{:S(2)}, u32[]{:S(2)}) collective-permute-start(bf16[24,2944]{1,0:T(8,128)(2,1)S(1)} %get-tuple-element.19), channel_id=1, source_target_pairs={{0,64},{16,80},{32,96},{48,112},{64,0},{80,16},{96,32},{112,48},{1... | collective-permute-start | bytes 423944 | tf_op jit(solution)/shard_map/ppermute | solution.py:219
  15.0 21.9 %collective-permute-start.4 = (bf16[24,2944]{1,0:T(8,128)(2,1)S(1)}, bf16[24,2944]{1,0:T(8,128)(2,1)S(1)}, u32[]{:S(2)}, u32[]{:S(2)}) collective-permute-start(bf16[24,2944]{1,0:T(8,128)(2,1)S(1)} %get-tuple-element.20), channel_id=1, source_target_pairs={{0,80},{16,96},{32,112},{48,0},{64,16},{80,32},{96,48},{112,64},{1... | collective-permute-start | bytes 423944 | tf_op jit(solution)/shard_map/ppermute | solution.py:219
  20.0 19.9 %collective-permute-start.5 = (bf16[24,2944]{1,0:T(8,128)(2,1)S(1)}, bf16[24,2944]{1,0:T(8,128)(2,1)S(1)}, u32[]{:S(2)}, u32[]{:S(2)}) collective-permute-start(bf16[24,2944]{1,0:T(8,128)(2,1)S(1)} %get-tuple-element.21), channel_id=1, source_target_pairs={{0,96},{16,112},{32,0},{48,16},{64,32},{80,48},{96,64},{112,80},{1... | collective-permute-start | bytes 423944 | tf_op jit(solution)/shard_map/ppermute | solution.py:219
  24.8 16.4 %collective-permute-start.6 = (bf16[24,2944]{1,0:T(8,128)(2,1)S(1)}, bf16[24,2944]{1,0:T(8,128)(2,1)S(1)}, u32[]{:S(2)}, u32[]{:S(2)}) collective-permute-start(bf16[24,2944]{1,0:T(8,128)(2,1)S(1)} %get-tuple-element.22), channel_id=1, source_target_pairs={{0,112},{16,0},{32,16},{48,32},{64,48},{80,64},{96,80},{112,96},{1... | collective-permute-start | bytes 423944 | tf_op jit(solution)/shard_map/ppermute | solution.py:219
  43.5 24.7 %copy-start.3 = (bf16[256,2880]{1,0:T(8,128)(2,1)}, bf16[256,2880]{1,0:T(8,128)(2,1)S(1)}, u32[]{:S(2)}) copy-start(bf16[256,2880]{1,0:T(8,128)(2,1)S(1)} %get-tuple-element.24) | copy-start | bytes 4423684
  68.2 6.1 %copy-start.13 = (s32[128]{0:T(128)S(1)}, s32[128]{0:T(128)}, u32[]{:S(2)}) copy-start(s32[128]{0:T(128)} %param.12) | copy-start | bytes 1540
  68.2 25.8 %all-to-all-start.1 = ((bf16[16,16,2880]{2,1,0:T(8,128)(2,1)}), bf16[16,16,2880]{2,1,0:T(8,128)(2,1)S(1)}, u32[]{:S(2)}, u32[]{:S(2)}) async-start(bf16[16,16,2880]{2,1,0:T(8,128)(2,1)} %bitcast.17), calls=%async_computation.1 | async-start | bytes 3014656 | tf_op jit(solution)/shard_map/all_to_all | solution.py:233
  74.9 76.5 %collective-permute-start.7 = (bf16[16,16,2944]{2,1,0:T(8,128)(2,1)S(1)}, bf16[16,16,2944]{2,1,0:T(8,128)(2,1)}, u32[]{:S(2)}, u32[]{:S(2)}) collective-permute-start(bf16[16,16,2944]{2,1,0:T(8,128)(2,1)S(1)} %all_to_all.20), channel_id=1, source_target_pairs={{0,128},{128,0},{1,129},{129,1},{2,130},{130,2},{3,131},{131,3},{4... | collective-permute-start | bytes 4521992 | tf_op jit(solution)/shard_map/ppermute | solution.py:223
  94.0 11.0 %copy-start = (bf16[16,16,2880]{2,1,0:T(8,128)(2,1)}, bf16[16,16,2880]{2,1,0:T(8,128)(2,1)S(1)}, u32[]{:S(2)}) copy-start(bf16[16,16,2880]{2,1,0:T(8,128)(2,1)S(1)} %all-to-all-done.1) | copy-start | bytes 4423684
  94.0 3.9 %copy-start.11 = (bf16[1,480,8640]{2,1,0:T(8,128)(2,1)S(1)}, bf16[1,480,8640]{2,1,0:T(8,128)(2,1)}, u32[]{:S(2)}) copy-start(bf16[1,480,8640]{2,1,0:T(8,128)(2,1)} %param.13) | copy-start | bytes 24883204
  105.0 1.1 copy-start.4
  107.7 43.7 %copy-start.10 = (s32[128]{0:T(128)S(1)}, s32[128]{0:T(128)}, u32[]{:S(2)}) copy-start(s32[128]{0:T(128)} %expert_ref.3) | copy-start | bytes 1540
  107.7 43.7 %all-to-all-start.2 = ((bf16[16,16,2880]{2,1,0:T(8,128)(2,1)}), bf16[16,16,2880]{2,1,0:T(8,128)(2,1)S(1)}, u32[]{:S(2)}, u32[]{:S(2)}) async-start(bf16[16,16,2880]{2,1,0:T(8,128)(2,1)} %bitcast.18), calls=%async_computation.2 | async-start | bytes 3014656 | tf_op jit(solution)/shard_map/all_to_all | solution.py:233
  113.9 37.5 %collective-permute-start.8 = (bf16[3,240,256]{2,1,0:T(8,128)(2,1)}, bf16[3,240,256]{2,1,0:T(8,128)(2,1)S(1)}, u32[]{:S(2)}, u32[]{:S(2)}) collective-permute-start(bf16[3,240,256]{2,1,0:T(8,128)(2,1)} %copy-done.12), channel_id=1, source_target_pairs={{0,128},{128,0},{1,129},{129,1},{2,130},{130,2},{3,131},{131,3},{4... | collective-permute-start | bytes 1105928 | tf_op jit(solution)/shard_map/ppermute | solution.py:223
  116.8 66.5 %collective-permute-start.9 = (bf16[16,16,2880]{2,1,0:T(8,128)(2,1)}, bf16[16,16,2880]{2,1,0:T(8,128)(2,1)}, u32[]{:S(2)}, u32[]{:S(2)}) collective-permute-start(bf16[16,16,2880]{2,1,0:T(8,128)(2,1)} %copy-done), channel_id=1, source_target_pairs={{0,128},{128,0},{1,129},{129,1},{2,130},{130,2},{3,131},{131,3},{4... | collective-permute-start | bytes 4423688 | tf_op jit(solution)/shard_map/ppermute | solution.py:223
  152.3 0.9 copy-start.2
  153.2 30.1 %copy-start.1 = (bf16[16,16,2880]{2,1,0:T(8,128)(2,1)S(1)}, bf16[16,16,2880]{2,1,0:T(8,128)(2,1)}, u32[]{:S(2)}) copy-start(bf16[16,16,2880]{2,1,0:T(8,128)(2,1)} %copy-done) | copy-start | bytes 4423684
  153.2 37.5 %all-to-all-start.3 = ((bf16[8,16,2880]{2,1,0:T(8,128)(2,1)}), bf16[8,16,2880]{2,1,0:T(8,128)(2,1)}, u32[]{:S(2)}, u32[]{:S(2)}) async-start(bf16[8,16,2880]{2,1,0:T(8,128)(2,1)} %copy-done.2), calls=%async_computation.3 | async-start | bytes 1507328 | tf_op jit(solution)/shard_map/all_to_all | solution.py:292
  183.3 1.0 copy-start.6
  (3 other events, 2.2 us)

commit v3 on v2

v3 whole, which is shorter than its diff:
```python
import jax
import jax.numpy as jnp
from jax import lax
from jax.experimental import pallas as pl
from jax.experimental.pallas import tpu as pltpu
from jax.sharding import Mesh, PartitionSpec as P

F32 = jnp.float32
BF16 = jnp.bfloat16
D = 2880
WIDE = 2944
EDGE = 2816
LAST = D - EDGE
TOKENS = 16
TOPK = 4
PLANES = 8
PEERS = 16
GROUP = 5
SLOTS = 2 * GROUP
PACKED = 24
ROWS = 256
GATHERED = PLANES * 16
UNITS = 480
HALF = 240
STEP = 512
PLANE = ("x", "y", "c")
ALL = ("dp", "z", "x", "y", "c")

VMEM = pl.BlockSpec(memory_space=pltpu.VMEM)
SMEM = pl.BlockSpec(memory_space=pltpu.SMEM)
WAITED = pl.BlockSpec(memory_space=pl.ANY)


def dot(left, right, left_dim, right_dim):
    return lax.dot_general(
        left, right, (((left_dim,), (right_dim,)), ((), ())), preferred_element_type=F32
    )


def chunks(total):
    return [(at, min(STEP, total - at)) for at in range(0, total, STEP)]


def iota(shape, dim):
    return lax.broadcasted_iota(jnp.int32, shape, dim)


def call(kernel, out_shape, in_specs, flops, moved, scratch=(), mib=24):
    outs = jax.tree.map(lambda _: VMEM, out_shape)
    return pl.pallas_call(
        kernel,
        out_shape=out_shape,
        in_specs=in_specs,
        out_specs=outs,
        scratch_shapes=list(scratch),
        compiler_params=pltpu.CompilerParams(vmem_limit_bytes=mib << 20),
        cost_estimate=pl.CostEstimate(flops=flops, bytes_accessed=moved, transcendentals=0),
    )


def shape(dims, kind=BF16):
    return jax.ShapeDtypeStruct(dims, kind)


def stage_kernel(token_ref, grad_ref, id_ref, prob_ref, out_ref):
    out_ref[:TOKENS, :EDGE] = token_ref[:, :EDGE]
    out_ref[TOKENS:, :EDGE] = grad_ref[:, :EDGE]
    lane = iota((TOKENS, 128), 1)
    blank = jnp.zeros((TOKENS, 128 - LAST), F32)
    tail = jnp.concatenate([token_ref[:, EDGE:].astype(F32), blank], axis=1)
    grad_tail = jnp.concatenate([grad_ref[:, EDGE:].astype(F32), blank], axis=1)
    prob = prob_ref[...]
    high = prob.astype(BF16).astype(F32)
    rest = prob - high
    middle = rest.astype(BF16).astype(F32)
    for at, part in enumerate((id_ref[...].astype(F32), high, middle, rest - middle)):
        for k in range(TOPK):
            tail = jnp.where(lane == LAST + TOPK * at + k, part[:, k : k + 1], tail)
    out_ref[:TOKENS, EDGE:] = tail.astype(BF16)
    out_ref[TOKENS:, EDGE:] = grad_tail.astype(BF16)


def pack_kernel(plane_ref, raw_ref, *refs):
    out_refs = refs[-PLANES:]
    routes = raw_ref[:TOKENS, EDGE:].astype(F32)

    def fact(at):
        return routes[:, LAST + at : LAST + at + TOPK]

    ids = fact(0).astype(jnp.int32)
    prob = fact(TOPK) + (fact(2 * TOPK) + fact(3 * TOPK))
    grid = (TOKENS, ROWS)
    row = iota(grid, 1)
    hop = (row * 2731) >> 16
    slot = row - PACKED * hop
    is_grad = slot >= SLOTS
    slot = jnp.where(is_grad, slot - SLOTS, slot)
    expert = GROUP * ((plane_ref[0] + hop) & (PLANES - 1)) + (slot >> 1)
    picked, weight = pick_tokens(ids, prob, expert, slot)
    scale = jnp.sum(picked * weight, axis=0, keepdims=True)
    scale = jnp.where(is_grad[:1], scale, 0.0)
    scale = jnp.broadcast_to(scale, (TOKENS, ROWS)).T[:, :1]
    want_grad = jnp.where(is_grad, 1.0, 0.0).T[:, :1] > 0.5
    picked = picked.T.astype(BF16)
    for at, size in chunks(WIDE):
        end = min(at + size, D)
        value = jnp.where(
            want_grad,
            scale * dot(picked, raw_ref[TOKENS:, at:end], 1, 0),
            dot(picked, raw_ref[:TOKENS, at:end], 1, 0),
        )
        if end < at + size:
            value = jnp.concatenate([value, jnp.zeros((ROWS, at + size - end), F32)], axis=1)
        for k, out_ref in enumerate(out_refs):
            out_ref[:, at : at + size] = value[PACKED * k : PACKED * (k + 1)].astype(BF16)


def pick_tokens(ids, prob, expert, slot):
    has = jnp.zeros(expert.shape, F32)
    weight = jnp.zeros(expert.shape, F32)
    for k in range(TOPK):
        match = ids[:, k : k + 1] == expert
        has = jnp.where(match, 1.0, has)
        weight = jnp.where(match, prob[:, k : k + 1], weight)
    square = (TOKENS, TOKENS)
    earlier = (iota(square, 1) < iota(square, 0)).astype(F32).astype(BF16)
    rank = dot(earlier, has.astype(BF16), 1, 0).astype(jnp.int32)
    wanted = (has > 0.5) & (rank == (slot & 1)) & (slot < SLOTS)
    return jnp.where(wanted, 1.0, 0.0), weight


def local_slot(expert_ref, plane_ref, row):
    local = jnp.zeros(row.shape, jnp.int32)
    for peer in range(PEERS):
        named = expert_ref[plane_ref[0] * PEERS + peer] - GROUP * plane_ref[0]
        local = jnp.where((row >> 4) == peer, named, local)
    return 2 * local + (row & 1)


def pick_kernel(expert_ref, plane_ref, *refs):
    blocks, out_ref = refs[:PLANES], refs[-1]
    grid = (ROWS, ROWS)
    row, column = iota(grid, 0), iota(grid, 1)
    source = PACKED * ((row >> 1) & (PLANES - 1)) + local_slot(expert_ref, plane_ref, row)
    column = column[:, : PLANES * PACKED]
    source = source[:, : PLANES * PACKED]
    pick_row = (column == source).astype(F32).astype(BF16)
    pick_grad = (column == source + SLOTS).astype(F32).astype(BF16)
    for at, size in chunks(WIDE):
        block = jnp.concatenate(
            [ref[:, at : at + size].astype(F32) for ref in blocks], axis=0
        ).astype(BF16)
        for first, picked in ((0, pick_row), (16, pick_grad)):
            value = dot(picked, block, 1, 0).astype(BF16)
            out_ref[:, first : first + 16, at : at + size] = value.reshape(PEERS, 16, size)


def token_part(ref, at=0, end=WIDE):
    return ref[:, :16, at:end].reshape(ROWS, end - at)


def grad_part(ref, at=0, end=D):
    return ref[:, 16:, at:end].reshape(ROWS, end - at)


def shifted(rows):
    return pltpu.roll(rows.astype(F32), LAST, 1).astype(BF16)


def unit_kernel(
    limit_ref, replica_ref, pair_ref, weight_ref, _, own_ref, other_ref, part_ref, shift_ref
):
    rows = token_part(pair_ref)
    shift_ref[...] = shifted(rows)
    gate = dot(weight_ref[:, :WIDE], rows, 1, 1)
    up = dot(weight_ref[:, EDGE : 2 * D], shift_ref[...], 1, 1)
    back = dot(weight_ref[:, 2 * D :], grad_part(pair_ref), 1, 1)
    mask = jnp.where(iota(gate.shape, 0) < limit_ref[0], 1.0, 0.0)
    sigma = jax.nn.sigmoid(gate)
    active = gate * sigma * mask
    hidden = (active * up).astype(BF16)
    grad_gate = (back * up * (sigma * (1.0 + gate * (1.0 - sigma))) * mask).astype(BF16)
    grad_up = (back * active).astype(BF16)
    for half in range(2):
        for target, mine in ((own_ref, half), (other_ref, 1 - half)):

            @pl.when(replica_ref[0] == mine)
            def _(target=target, at=half * HALF):
                target[0] = grad_gate[at : at + HALF]
                target[1] = grad_up[at : at + HALF]
                target[2] = hidden[at : at + HALF]

    gate_rows = grad_gate.astype(F32).T.astype(BF16)
    up_rows = grad_up.astype(F32).T.astype(BF16)
    for at, size in chunks(WIDE):
        end = at + size
        value = dot(gate_rows, weight_ref[:, at:end], 1, 0)
        wide = dot(up_rows, weight_ref[:, EDGE + at : min(EDGE + end + 128, 2 * D)], 1, 0)
        value = value + pltpu.roll(wide, wide.shape[1] - LAST, 1)[:, :size]
        keep = min(end, D) - at
        part_ref[:, at : at + keep] = value[:, :keep].astype(BF16)


def weight_kernel(own_ref, other_ref, pair_ref, far_ref, out_ref, shift_ref, far_shift_ref):
    shift_ref[...] = shifted(token_part(pair_ref))
    far_shift_ref[...] = shifted(token_part(far_ref))

    def term(which, near, far):
        return dot(own_ref[which], near, 1, 0) + dot(other_ref[which], far, 1, 0)

    def gate_term(at, end):
        return term(0, token_part(pair_ref, at, end), token_part(far_ref, at, end))

    def up_term(at, end):
        return term(1, shift_ref[:, at:end], far_shift_ref[:, at:end])

    for at, size in chunks(EDGE):
        value = gate_term(at, at + size)
        out_ref[0, :, at : at + size] = value.astype(BF16)
    value = gate_term(EDGE, WIDE) + up_term(0, 128)
    out_ref[0, :, EDGE:WIDE] = value.astype(BF16)
    for at, size in chunks(WIDE - 128):
        value = up_term(128 + at, 128 + at + size)
        out_ref[0, :, WIDE + at : WIDE + at + size] = value.astype(BF16)
    for at, size in chunks(D):
        value = term(
            2, grad_part(pair_ref, at, at + size), grad_part(far_ref, at, at + size)
        )
        out_ref[0, :, 2 * D + at : 2 * D + at + size] = value.astype(BF16)


def gather_kernel(expert_ref, plane_ref, part_ref, *out_refs):
    grid = (GATHERED, ROWS)
    row, column = iota(grid, 0), iota(grid, 1)
    same_hop = (row >> 4) == ((column >> 1) & (PLANES - 1))
    same_slot = (row & 15) == local_slot(expert_ref, plane_ref, column)
    picked = (same_hop & same_slot).astype(F32).astype(BF16)
    for at, size in chunks(D):
        value = dot(picked, part_ref[:, at : at + size], 1, 0).astype(BF16)
        for k, out_ref in enumerate(out_refs):
            out_ref[:, at : at + size] = value[16 * k : 16 * (k + 1)]


def sum_kernel(plane_ref, id_ref, *refs):
    blocks, out_ref = refs[:PLANES], refs[PLANES]
    row = iota((TOKENS, GATHERED), 1)
    slot = row & 15
    expert = GROUP * ((plane_ref[0] + (row >> 4)) & (PLANES - 1)) + (slot >> 1)
    picked, _ = pick_tokens(id_ref[...], jnp.zeros((TOKENS, TOPK), F32), expert, slot)
    picked = picked.astype(BF16)
    for at, size in chunks(D):
        block = jnp.concatenate([ref[:, at : at + size] for ref in blocks], axis=0)
        out_ref[:, at : at + size] = dot(picked, block, 1, 0).astype(BF16)


def along_z(value, by):
    return lax.ppermute(value, "z", [(i, (i + by) % PLANES) for i in range(PLANES)])


def swap_dp(value):
    return lax.ppermute(value, "dp", [(0, 1), (1, 0)])


def after(value, other):
    return pl.pallas_call(
        lambda *refs: None,
        out_shape=shape(value.shape),
        in_specs=[WAITED, WAITED],
        out_specs=WAITED,
        input_output_aliases={0: 0},
    )(value, other)


def in_plane(blocks):
    return lax.all_to_all(blocks, PLANE, split_axis=0, concat_axis=0, tiled=True)


FAR_FIRST = (4, 3, 5, 2, 6, 1, 7)


def to_planes(blocks):
    sent = {by: along_z(blocks[by], by) for by in FAR_FIRST}
    return [blocks[0]] + [sent[by] for by in range(1, PLANES)]


def shards(tokens, grad_out, route_ids, route_prob, device_expert, unit_count, expert_weights):
    plane = lax.axis_index("z").astype(jnp.int32)
    replica = lax.axis_index("dp").astype(jnp.int32).reshape(1)
    limit = lax.dynamic_slice_in_dim(unit_count, plane * PEERS + lax.axis_index(PLANE), 1)
    slot_weights = expert_weights[0]

    plane = plane.reshape(1)
    row_flops = 2 * ROWS * D
    raw = call(stage_kernel, shape((2 * TOKENS, WIDE)), [VMEM] * 4, 0, 400_000, (), 8)(
        tokens, grad_out, route_ids, route_prob
    )

    def pack(block):
        return call(
            pack_kernel,
            [shape((PACKED, WIDE))] * PLANES,
            [SMEM, VMEM],
            row_flops * TOKENS,
            1_400_000,
            (),
            12,
        )(plane, block)

    def pick(blocks, *earlier):
        return call(
            pick_kernel,
            shape((PEERS, 32, WIDE)),
            [SMEM, SMEM] + [VMEM] * PLANES + [WAITED] * len(earlier),
            2 * row_flops * PLANES * PACKED,
            4_200_000,
            (),
            14,
        )(device_expert, plane, *blocks, *earlier)

    blocks = pack(raw)
    far_blocks = pack(swap_dp(raw))
    pairs = in_plane(pick(to_planes(blocks), far_blocks[0]))
    far_sent = pick(to_planes(far_blocks))

    own, other, part = call(
        unit_kernel,
        (shape((3, HALF, ROWS)), shape((3, HALF, ROWS)), shape((ROWS, D))),
        [SMEM, SMEM, VMEM, VMEM, WAITED],
        5 * row_flops * UNITS,
        14_000_000,
        [pltpu.VMEM((ROWS, WIDE), BF16)],
        28,
    )(limit, replica, pairs, slot_weights, far_sent)
    other = swap_dp(other)

    returned = in_plane(part.reshape(PEERS, 16, D)).reshape(ROWS, D)
    token_parts = call(
        gather_kernel,
        [shape((16, D))] * PLANES,
        [SMEM, SMEM, VMEM],
        row_flops * GATHERED,
        2_400_000,
    )(device_expert, plane, returned)
    home = {by: along_z(token_parts[by], -by) for by in FAR_FIRST}
    home = [token_parts[0]] + [home[by] for by in range(1, PLANES)]
    far_pairs = in_plane(after(far_sent, returned))
    grad_weights = call(
        weight_kernel,
        shape((1, HALF, 3 * D)),
        [VMEM] * 4,
        3 * row_flops * UNITS,
        12_000_000,
        [pltpu.VMEM((ROWS, WIDE), BF16)] * 2,
        24,
    )(own, other, pairs, far_pairs)
    grad_tokens = call(
        sum_kernel, shape((TOKENS, D)), [SMEM] + [VMEM] * (1 + PLANES), row_flops, 900_000
    )(plane, route_ids, *home)
    return grad_tokens, grad_weights


def solution(mesh):
    fine = Mesh(mesh.devices.reshape(2, PLANES, 4, 2, 2), ALL)
    slots = ("z",) + PLANE
    in_specs = (P(ALL), P(ALL), P(ALL), P(ALL), P(), P(), P(slots))
    out_specs = (P(ALL), P(slots, "dp"))
    return jax.shard_map(shards, mesh=fine, in_specs=in_specs, out_specs=out_specs, check_vma=False)
```

time: 195 us -> 191 us (0.979)
  waiting for transfers between devices: 91.3 us -> 55.6 us
  starting transfers between devices: 43.8 us -> 67.1 us
  Pallas kernels: 19.4 us -> 25.6 us
  local copies, waits for them, and re-layouts: 12.9 us -> 16.8 us
    ppermute x3 -> x2, waiting for transfers between devices: 58.9 us -> 12.8 us  [swap_dp(): return lax.ppermute(value, 'dp', [(0, 1), (1, 0)])]
    ppermute x7 -> x21, starting transfers between devices: 19.8 us -> 49.9 us  [along_z(): lax.ppermute(value, 'z', [(i, (i + by) % PLANES) for i in range(PLANES)])]
    ppermute x7 -> x21, waiting for transfers between devices: 16.2 us -> 42.8 us  [along_z(): lax.ppermute(value, 'z', [(i, (i + by) % PLANES) for i in range(PLANES)])]
    all_to_all x2, waiting for transfers between devices: 16.2 us -> 0.01 us  [in_plane(): lax.all_to_all(blocks, PLANE, split_axis=0, concat_axis=0, tiled=True)]
    all_to_all x1 -> x0, starting transfers between devices: 5.2 us -> none  [shards(): lax.all_to_all(token_parts, 'z', split_axis=0, concat_axis=0, tiled=True)]
    pallas_call x5 -> x9, Pallas kernels: 12.4 us -> 16.8 us  [the longest x1 7.33 us: shards(): call(weight_kernel, shape((1, HALF, 3 * D)), [VMEM] * 4, 3 * row_flops *...]
    unnamed x30 -> x42, local copies, waits for them, and re-layouts: 12.4 us -> 16.3 us
    ppermute x3 -> x2, starting transfers between devices: 6.43 us -> 5.21 us  [swap_dp(): return lax.ppermute(value, 'dp', [(0, 1), (1, 0)])]
  transfers between devices with their start and end apart: 13 -> 25, of which waited for: 8 -> 15; matrix products, arithmetic and copies ran while one was open for 0% -> 0% of each run, Pallas kernels for 7% -> 3%
where the time goes in v3:
time: 191 us
  starting transfers between devices  67.1 us (35%)
  waiting for transfers between devices  55.6 us (29%)
  Pallas kernels  25.6 us (13%)
  blocking collectives  24.6 us (13%)
  local copies, waits for them, and re-layouts  16.8 us (9%)
    ppermute x21, starting transfers between devices, along_z(): lax.ppermute(value, 'z', [(i, (i + by) % PLANES) for i in range(PLANES)])  49.9 us
    ppermute x21, waiting for transfers between devices, along_z(): lax.ppermute(value, 'z', [(i, (i + by) % PLANES) for i in range(PLANES)])  42.8 us
    all_to_all x1, blocking collectives, in_plane(): lax.all_to_all(blocks, PLANE, split_axis=0, concat_axis=0, tiled=True)  24.6 us
    unnamed x42, local copies, waits for them, and re-layouts  16.3 us
    ppermute x2, waiting for transfers between devices, swap_dp(): return lax.ppermute(value, 'dp', [(0, 1), (1, 0)])  12.8 us
    all_to_all x2, starting transfers between devices, in_plane(): lax.all_to_all(blocks, PLANE, split_axis=0, concat_axis=0, tiled=True)  11.9 us
    pallas_call x1, Pallas kernels, shards(): call(unit_kernel, (shape((3, HALF, ROWS)), shape((3, HALF, ROWS)), shape(...  8.83 us
    pallas_call x1, Pallas kernels, shards(): call(weight_kernel, shape((1, HALF, 3 * D)), [VMEM] * 4, 3 * row_flops *...  7.33 us
  transfers between devices with their start and end apart: 25, of which 15 were waited for; matrix products, arithmetic and copies ran while one was open for 0% of the time, Pallas kernels for 3%

profile of v3, /device:TPU:2, one launch (start us, length us, event | category | flops | bytes accessed | tf_op | source)
XLA Modules:
  0.0 190.6 jit_solution(18279395181290208080)
XLA Ops:
  4.0 3.3 %collective-permute-start.7 = (bf16[32,2944]{1,0:T(8,128)(2,1)S(1)}, bf16[32,2944]{1,0:T(8,128)(2,1)S(1)}, u32[]{:S(2)}, u32[]{:S(2)}) collective-permute-start(bf16[32,2944]{1,0:T(8,128)(2,1)S(1)} %shard_map.86.raw_ref), channel_id=1, source_target_pairs={{0,128},{128,0},{1,129},{129,1},{2,130},{130,2},{3,131},{131,3},{4... | collective-permute-start | bytes 565256 | tf_op jit(solution)/shard_map/ppermute | solution.py:261
  10.6 3.3 %collective-permute-start.1 = (bf16[24,2944]{1,0:T(8,128)(2,1)S(1)}, bf16[24,2944]{1,0:T(8,128)(2,1)S(1)}, u32[]{:S(2)}, u32[]{:S(2)}) collective-permute-start(bf16[24,2944]{1,0:T(8,128)(2,1)S(1)} %get-tuple-element.31), channel_id=1, source_target_pairs={{0,32},{16,48},{32,64},{48,80},{64,96},{80,112},{96,0},{112,16},{1... | collective-permute-start | bytes 423944 | tf_op jit(solution)/shard_map/ppermute | solution.py:257
  13.8 4.0 %collective-permute-start.2 = (bf16[24,2944]{1,0:T(8,128)(2,1)S(1)}, bf16[24,2944]{1,0:T(8,128)(2,1)S(1)}, u32[]{:S(2)}, u32[]{:S(2)}) collective-permute-start(bf16[24,2944]{1,0:T(8,128)(2,1)S(1)} %get-tuple-element.32), channel_id=1, source_target_pairs={{0,48},{16,64},{32,80},{48,96},{64,112},{80,0},{96,16},{112,32},{1... | collective-permute-start | bytes 423944 | tf_op jit(solution)/shard_map/ppermute | solution.py:257
  19.9 3.4 %collective-permute-start.4 = (bf16[24,2944]{1,0:T(8,128)(2,1)S(1)}, bf16[24,2944]{1,0:T(8,128)(2,1)S(1)}, u32[]{:S(2)}, u32[]{:S(2)}) collective-permute-start(bf16[24,2944]{1,0:T(8,128)(2,1)S(1)} %get-tuple-element.34), channel_id=1, source_target_pairs={{0,80},{16,96},{32,112},{48,0},{64,16},{80,32},{96,48},{112,64},{1... | collective-permute-start | bytes 423944 | tf_op jit(solution)/shard_map/ppermute | solution.py:257
  23.4 5.6 %collective-permute-done.1.refs_2_ = bf16[24,2944]{1,0:T(8,128)(2,1)S(1)} collective-permute-done((bf16[24,2944]{1,0:T(8,128)(2,1)S(1)}, bf16[24,2944]{1,0:T(8,128)(2,1)S(1)}, u32[]{:S(2)}, u32[]{:S(2)}) %collective-permute-start.1) | collective-permute-done | bytes 141344 | tf_op jit(solution)/shard_map/ppermute | solution.py:257
  29.5 3.8 %collective-permute-start.6 = (bf16[24,2944]{1,0:T(8,128)(2,1)S(1)}, bf16[24,2944]{1,0:T(8,128)(2,1)S(1)}, u32[]{:S(2)}, u32[]{:S(2)}) collective-permute-start(bf16[24,2944]{1,0:T(8,128)(2,1)S(1)} %get-tuple-element.36), channel_id=1, source_target_pairs={{0,112},{16,0},{32,16},{48,32},{64,48},{80,64},{96,80},{112,96},{1... | collective-permute-start | bytes 423944 | tf_op jit(solution)/shard_map/ppermute | solution.py:257
  36.9 3.0 %collective-permute-done.4.refs_5_ = bf16[24,2944]{1,0:T(8,128)(2,1)S(1)} collective-permute-done((bf16[24,2944]{1,0:T(8,128)(2,1)S(1)}, bf16[24,2944]{1,0:T(8,128)(2,1)S(1)}, u32[]{:S(2)}, u32[]{:S(2)}) %collective-permute-start.4) | collective-permute-done | bytes 141344 | tf_op jit(solution)/shard_map/ppermute | solution.py:257
  39.9 3.0 %collective-permute-done.5.refs_6_ = bf16[24,2944]{1,0:T(8,128)(2,1)S(1)} collective-permute-done((bf16[24,2944]{1,0:T(8,128)(2,1)S(1)}, bf16[24,2944]{1,0:T(8,128)(2,1)S(1)}, u32[]{:S(2)}, u32[]{:S(2)}) %collective-permute-start.5) | collective-permute-done | bytes 141344 | tf_op jit(solution)/shard_map/ppermute | solution.py:257
  45.2 3.3 %shard_map.89 = bf16[16,32,2944]{2,1,0:T(8,128)(2,1)} custom-call(s32[128]{0:T(128)S(1)} %copy-done.15, s32[1]{0:T(128)} %bitcast.plane_ref, bf16[24,2944]{1,0:T(8,128)(2,1)S(1)} %get-tuple-element.29.refs_0_, bf16[24,2944]{1,0:T(8,128)(2,1)S(1)} %collective-permute-done.refs_1_, bf16[24,2944]{1,0:T(8,128)(2,1)S(1)} %collective-permute-done.1.refs_2_, ...), custom_call_target="tpu_custom_call" | custom-call | flops 566231040 | bytes 4200000 | tf_op jit(solution)/shard_map/pallas_call | solution.py:310
  48.5 5.1 %all-to-all-start = ((bf16[16,32,2944]{2,1,0:T(8,128)(2,1)}), bf16[16,32,2944]{2,1,0:T(8,128)(2,1)}, u32[]{:S(2)}, u32[]{:S(2)}) async-start(bf16[16,32,2944]{2,1,0:T(8,128)(2,1)} %shard_map.89), calls=%async_computation | async-start | bytes 6029312 | tf_op jit(solution)/shard_map/all_to_all | solution.py:275
  58.2 4.7 %collective-permute-start.11 = (bf16[24,2944]{1,0:T(8,128)(2,1)S(1)}, bf16[24,2944]{1,0:T(8,128)(2,1)S(1)}, u32[]{:S(2)}, u32[]{:S(2)}) collective-permute-start(bf16[24,2944]{1,0:T(8,128)(2,1)S(1)} %get-tuple-element.41), channel_id=1, source_target_pairs={{0,64},{16,80},{32,96},{48,112},{64,0},{80,16},{96,32},{112,48},{1... | collective-permute-start | bytes 423944 | tf_op jit(solution)/shard_map/ppermute | solution.py:257
  66.8 7.9 %collective-permute-done.9.refs_2_ = bf16[24,2944]{1,0:T(8,128)(2,1)S(1)} collective-permute-done((bf16[24,2944]{1,0:T(8,128)(2,1)S(1)}, bf16[24,2944]{1,0:T(8,128)(2,1)S(1)}, u32[]{:S(2)}, u32[]{:S(2)}) %collective-permute-start.9) | collective-permute-done | bytes 141344 | tf_op jit(solution)/shard_map/ppermute | solution.py:257
  76.0 3.9 %collective-permute-done.11.refs_4_ = bf16[24,2944]{1,0:T(8,128)(2,1)S(1)} collective-permute-done((bf16[24,2944]{1,0:T(8,128)(2,1)S(1)}, bf16[24,2944]{1,0:T(8,128)(2,1)S(1)}, u32[]{:S(2)}, u32[]{:S(2)}) %collective-permute-start.11) | collective-permute-done | bytes 141344 | tf_op jit(solution)/shard_map/ppermute | solution.py:257
  81.3 4.2 %collective-permute-done.13.refs_6_ = bf16[24,2944]{1,0:T(8,128)(2,1)S(1)} collective-permute-done((bf16[24,2944]{1,0:T(8,128)(2,1)S(1)}, bf16[24,2944]{1,0:T(8,128)(2,1)S(1)}, u32[]{:S(2)}, u32[]{:S(2)}) %collective-permute-start.13) | collective-permute-done | bytes 141344 | tf_op jit(solution)/shard_map/ppermute | solution.py:257
  95.2 4.4 %copy-done.2 = bf16[1,480,8640]{2,1,0:T(8,128)(2,1)S(1)} copy-done((bf16[1,480,8640]{2,1,0:T(8,128)(2,1)S(1)}, bf16[1,480,8640]{2,1,0:T(8,128)(2,1)}, u32[]{:S(2)}) %copy-start.2) | copy-done | bytes 8294424
  99.6 8.8 %shard_map.91 = (bf16[3,240,256]{2,1,0:T(8,128)(2,1)S(1)}, bf16[3,240,256]{2,1,0:T(8,128)(2,1)S(1)}, bf16[256,2880]{1,0:T(8,128)(2,1)S(1)}) custom-call(s32[1]{0:T(128)} %dynamic_slice.3.limit_ref, s32[1]{0:T(128)} %bitcast.1.replica_ref, bf16[16,32,2944]{2,1,0:T(8,128)(2,1)} %all-to-all-done.pair_ref, bf16[480,8640]{1,0:T(8,128)(2,1)S(1)} %bitcast.7, ...), custom_call_target="tpu_custom_call" | custom-call | flops 3538944000 | bytes 14000000 | tf_op jit(solution)/shard_map/pallas_call | solution.py:325
  108.5 24.6 %all_to_all.15 = bf16[16,16,2880]{2,1,0:T(8,128)(2,1)} all-to-all(bf16[16,16,2880]{2,1,0:T(8,128)(2,1)S(1)} %bitcast.8), channel_id=1, replica_groups=mesh['dp'=2,'z'=8,'x'=4,'y'=2,'c'=2] {'x','y','c'}, dimensions={0} | all-to-all | bytes 2949120 | tf_op jit(solution)/shard_map/all_to_all | solution.py:275
  133.1 6.9 %all-to-all-start.2 = ((bf16[16,32,2944]{2,1,0:T(8,128)(2,1)}), bf16[16,32,2944]{2,1,0:T(8,128)(2,1)}, u32[]{:S(2)}, u32[]{:S(2)}) async-start(bf16[16,32,2944]{2,1,0:T(8,128)(2,1)} %shard_map.94), calls=%async_computation.2 | async-start | bytes 6029312 | tf_op jit(solution)/shard_map/all_to_all | solution.py:275
  148.2 4.2 %collective-permute-start.18 = (bf16[16,2880]{1,0:T(8,128)(2,1)S(1)}, bf16[16,2880]{1,0:T(8,128)(2,1)S(1)}, u32[]{:S(2)}, u32[]{:S(2)}) collective-permute-start(bf16[16,2880]{1,0:T(8,128)(2,1)S(1)} %get-tuple-element.50), channel_id=1, source_target_pairs={{0,64},{16,80},{32,96},{48,112},{64,0},{80,16},{96,32},{112,48},{1... | collective-permute-start | bytes 276488 | tf_op jit(solution)/shard_map/ppermute | solution.py:257
  154.7 3.8 %collective-permute-start.20 = (bf16[16,2880]{1,0:T(8,128)(2,1)S(1)}, bf16[16,2880]{1,0:T(8,128)(2,1)S(1)}, u32[]{:S(2)}, u32[]{:S(2)}) collective-permute-start(bf16[16,2880]{1,0:T(8,128)(2,1)S(1)} %get-tuple-element.52), channel_id=1, source_target_pairs={{0,32},{16,48},{32,64},{48,80},{64,96},{80,112},{96,0},{112,16},{1... | collective-permute-start | bytes 276488 | tf_op jit(solution)/shard_map/ppermute | solution.py:257
  158.4 3.4 %collective-permute-done.17.refs_3_ = bf16[16,2880]{1,0:T(8,128)(2,1)S(1)} collective-permute-done((bf16[16,2880]{1,0:T(8,128)(2,1)S(1)}, bf16[16,2880]{1,0:T(8,128)(2,1)S(1)}, u32[]{:S(2)}, u32[]{:S(2)}) %collective-permute-start.17) | collective-permute-done | bytes 92192 | tf_op jit(solution)/shard_map/ppermute | solution.py:257
  161.8 3.5 %collective-permute-start.21 = (bf16[16,2880]{1,0:T(8,128)(2,1)S(1)}, bf16[16,2880]{1,0:T(8,128)(2,1)S(1)}, u32[]{:S(2)}, u32[]{:S(2)}) collective-permute-start(bf16[16,2880]{1,0:T(8,128)(2,1)S(1)} %get-tuple-element.53), channel_id=1, source_target_pairs={{0,16},{16,32},{32,48},{48,64},{64,80},{80,96},{96,112},{112,0},{1... | collective-permute-start | bytes 276488 | tf_op jit(solution)/shard_map/ppermute | solution.py:257
  170.4 12.8 %collective-permute-done.22.other_ref = bf16[3,240,256]{2,1,0:T(8,128)(2,1)S(1)} collective-permute-done((bf16[3,240,256]{2,1,0:T(8,128)(2,1)S(1)}, bf16[3,240,256]{2,1,0:T(8,128)(2,1)S(1)}, u32[]{:S(2)}, u32[]{:S(2)}) %collective-permute-start.22) | collective-permute-done | bytes 368672 | tf_op jit(solution)/shard_map/ppermute | solution.py:261
  183.2 7.3 %shard_map.95 = bf16[1,240,8640]{2,1,0:T(8,128)(2,1)} custom-call(bf16[3,240,256]{2,1,0:T(8,128)(2,1)S(1)} %get-tuple-element.54.own_ref, bf16[3,240,256]{2,1,0:T(8,128)(2,1)S(1)} %collective-permute-done.22.other_ref, bf16[16,32,2944]{2,1,0:T(8,128)(2,1)} %all-to-all-done.pair_ref, bf16[16,32,2944]{2,1,0:T(8,128)(2,1)} %all-to-all-done.2.far_ref), custom_call_target="tpu_custom_call" | custom-call | flops 2123366400 | bytes 12000000 | tf_op jit(solution)/shard_map/pallas_call | solution.py:347
  (80 shorter events, 51.6 us)
Async XLA Ops:
  4.0 25.5 %collective-permute-start.7 = (bf16[32,2944]{1,0:T(8,128)(2,1)S(1)}, bf16[32,2944]{1,0:T(8,128)(2,1)S(1)}, u32[]{:S(2)}, u32[]{:S(2)}) collective-permute-start(bf16[32,2944]{1,0:T(8,128)(2,1)S(1)} %shard_map.86.raw_ref), channel_id=1, source_target_pairs={{0,128},{128,0},{1,129},{129,1},{2,130},{130,2},{3,131},{131,3},{4... | collective-permute-start | bytes 565256 | tf_op jit(solution)/shard_map/ppermute | solution.py:261
  8.6 11.4 %collective-permute-start = (bf16[24,2944]{1,0:T(8,128)(2,1)S(1)}, bf16[24,2944]{1,0:T(8,128)(2,1)S(1)}, u32[]{:S(2)}, u32[]{:S(2)}) collective-permute-start(bf16[24,2944]{1,0:T(8,128)(2,1)S(1)} %get-tuple-element.30), channel_id=1, source_target_pairs={{0,16},{16,32},{32,48},{48,64},{64,80},{80,96},{96,112},{112,0},{1... | collective-permute-start | bytes 423944 | tf_op jit(solution)/shard_map/ppermute | solution.py:257
  10.6 18.4 %collective-permute-start.1 = (bf16[24,2944]{1,0:T(8,128)(2,1)S(1)}, bf16[24,2944]{1,0:T(8,128)(2,1)S(1)}, u32[]{:S(2)}, u32[]{:S(2)}) collective-permute-start(bf16[24,2944]{1,0:T(8,128)(2,1)S(1)} %get-tuple-element.31), channel_id=1, source_target_pairs={{0,32},{16,48},{32,64},{48,80},{64,96},{80,112},{96,0},{112,16},{1... | collective-permute-start | bytes 423944 | tf_op jit(solution)/shard_map/ppermute | solution.py:257
  13.8 23.1 %collective-permute-start.2 = (bf16[24,2944]{1,0:T(8,128)(2,1)S(1)}, bf16[24,2944]{1,0:T(8,128)(2,1)S(1)}, u32[]{:S(2)}, u32[]{:S(2)}) collective-permute-start(bf16[24,2944]{1,0:T(8,128)(2,1)S(1)} %get-tuple-element.32), channel_id=1, source_target_pairs={{0,48},{16,64},{32,80},{48,96},{64,112},{80,0},{96,16},{112,32},{1... | collective-permute-start | bytes 423944 | tf_op jit(solution)/shard_map/ppermute | solution.py:257
  17.9 19.0 %collective-permute-start.3 = (bf16[24,2944]{1,0:T(8,128)(2,1)S(1)}, bf16[24,2944]{1,0:T(8,128)(2,1)S(1)}, u32[]{:S(2)}, u32[]{:S(2)}) collective-permute-start(bf16[24,2944]{1,0:T(8,128)(2,1)S(1)} %get-tuple-element.33), channel_id=1, source_target_pairs={{0,64},{16,80},{32,96},{48,112},{64,0},{80,16},{96,32},{112,48},{1... | collective-permute-start | bytes 423944 | tf_op jit(solution)/shard_map/ppermute | solution.py:257
  19.9 19.9 %collective-permute-start.4 = (bf16[24,2944]{1,0:T(8,128)(2,1)S(1)}, bf16[24,2944]{1,0:T(8,128)(2,1)S(1)}, u32[]{:S(2)}, u32[]{:S(2)}) collective-permute-start(bf16[24,2944]{1,0:T(8,128)(2,1)S(1)} %get-tuple-element.34), channel_id=1, source_target_pairs={{0,80},{16,96},{32,112},{48,0},{64,16},{80,32},{96,48},{112,64},{1... | collective-permute-start | bytes 423944 | tf_op jit(solution)/shard_map/ppermute | solution.py:257
  28.9 13.9 %collective-permute-start.5 = (bf16[24,2944]{1,0:T(8,128)(2,1)S(1)}, bf16[24,2944]{1,0:T(8,128)(2,1)S(1)}, u32[]{:S(2)}, u32[]{:S(2)}) collective-permute-start(bf16[24,2944]{1,0:T(8,128)(2,1)S(1)} %get-tuple-element.35), channel_id=1, source_target_pairs={{0,96},{16,112},{32,0},{48,16},{64,32},{80,48},{96,64},{112,80},{1... | collective-permute-start | bytes 423944 | tf_op jit(solution)/shard_map/ppermute | solution.py:257
  29.5 15.0 %collective-permute-start.6 = (bf16[24,2944]{1,0:T(8,128)(2,1)S(1)}, bf16[24,2944]{1,0:T(8,128)(2,1)S(1)}, u32[]{:S(2)}, u32[]{:S(2)}) collective-permute-start(bf16[24,2944]{1,0:T(8,128)(2,1)S(1)} %get-tuple-element.36), channel_id=1, source_target_pairs={{0,112},{16,0},{32,16},{48,32},{64,48},{80,64},{96,80},{112,96},{1... | collective-permute-start | bytes 423944 | tf_op jit(solution)/shard_map/ppermute | solution.py:257
  48.5 46.6 %all-to-all-start = ((bf16[16,32,2944]{2,1,0:T(8,128)(2,1)}), bf16[16,32,2944]{2,1,0:T(8,128)(2,1)}, u32[]{:S(2)}, u32[]{:S(2)}) async-start(bf16[16,32,2944]{2,1,0:T(8,128)(2,1)} %shard_map.89), calls=%async_computation | async-start | bytes 6029312 | tf_op jit(solution)/shard_map/all_to_all | solution.py:275
  53.6 11.5 %collective-permute-start.8 = (bf16[24,2944]{1,0:T(8,128)(2,1)S(1)}, bf16[24,2944]{1,0:T(8,128)(2,1)S(1)}, u32[]{:S(2)}, u32[]{:S(2)}) collective-permute-start(bf16[24,2944]{1,0:T(8,128)(2,1)S(1)} %get-tuple-element.38), channel_id=1, source_target_pairs={{0,16},{16,32},{32,48},{48,64},{64,80},{80,96},{96,112},{112,0},{1... | collective-permute-start | bytes 423944 | tf_op jit(solution)/shard_map/ppermute | solution.py:257
  56.5 18.3 %collective-permute-start.9 = (bf16[24,2944]{1,0:T(8,128)(2,1)S(1)}, bf16[24,2944]{1,0:T(8,128)(2,1)S(1)}, u32[]{:S(2)}, u32[]{:S(2)}) collective-permute-start(bf16[24,2944]{1,0:T(8,128)(2,1)S(1)} %get-tuple-element.39), channel_id=1, source_target_pairs={{0,32},{16,48},{32,64},{48,80},{64,96},{80,112},{96,0},{112,16},{1... | collective-permute-start | bytes 423944 | tf_op jit(solution)/shard_map/ppermute | solution.py:257
  57.6 17.7 %collective-permute-start.10 = (bf16[24,2944]{1,0:T(8,128)(2,1)S(1)}, bf16[24,2944]{1,0:T(8,128)(2,1)S(1)}, u32[]{:S(2)}, u32[]{:S(2)}) collective-permute-start(bf16[24,2944]{1,0:T(8,128)(2,1)S(1)} %get-tuple-element.40), channel_id=1, source_target_pairs={{0,48},{16,64},{32,80},{48,96},{64,112},{80,0},{96,16},{112,32},{1... | collective-permute-start | bytes 423944 | tf_op jit(solution)/shard_map/ppermute | solution.py:257
  58.2 21.7 %collective-permute-start.11 = (bf16[24,2944]{1,0:T(8,128)(2,1)S(1)}, bf16[24,2944]{1,0:T(8,128)(2,1)S(1)}, u32[]{:S(2)}, u32[]{:S(2)}) collective-permute-start(bf16[24,2944]{1,0:T(8,128)(2,1)S(1)} %get-tuple-element.41), channel_id=1, source_target_pairs={{0,64},{16,80},{32,96},{48,112},{64,0},{80,16},{96,32},{112,48},{1... | collective-permute-start | bytes 423944 | tf_op jit(solution)/shard_map/ppermute | solution.py:257
  62.9 17.7 %collective-permute-start.12 = (bf16[24,2944]{1,0:T(8,128)(2,1)S(1)}, bf16[24,2944]{1,0:T(8,128)(2,1)S(1)}, u32[]{:S(2)}, u32[]{:S(2)}) collective-permute-start(bf16[24,2944]{1,0:T(8,128)(2,1)S(1)} %get-tuple-element.42), channel_id=1, source_target_pairs={{0,80},{16,96},{32,112},{48,0},{64,16},{80,32},{96,48},{112,64},{1... | collective-permute-start | bytes 423944 | tf_op jit(solution)/shard_map/ppermute | solution.py:257
  65.1 20.3 %collective-permute-start.13 = (bf16[24,2944]{1,0:T(8,128)(2,1)S(1)}, bf16[24,2944]{1,0:T(8,128)(2,1)S(1)}, u32[]{:S(2)}, u32[]{:S(2)}) collective-permute-start(bf16[24,2944]{1,0:T(8,128)(2,1)S(1)} %get-tuple-element.43), channel_id=1, source_target_pairs={{0,96},{16,112},{32,0},{48,16},{64,32},{80,48},{96,64},{112,80},{1... | collective-permute-start | bytes 423944 | tf_op jit(solution)/shard_map/ppermute | solution.py:257
  74.8 13.5 %collective-permute-start.14 = (bf16[24,2944]{1,0:T(8,128)(2,1)S(1)}, bf16[24,2944]{1,0:T(8,128)(2,1)S(1)}, u32[]{:S(2)}, u32[]{:S(2)}) collective-permute-start(bf16[24,2944]{1,0:T(8,128)(2,1)S(1)} %get-tuple-element.44), channel_id=1, source_target_pairs={{0,112},{16,0},{32,16},{48,32},{64,48},{80,64},{96,80},{112,96},{1... | collective-permute-start | bytes 423944 | tf_op jit(solution)/shard_map/ppermute | solution.py:257
  133.1 50.1 %all-to-all-start.2 = ((bf16[16,32,2944]{2,1,0:T(8,128)(2,1)}), bf16[16,32,2944]{2,1,0:T(8,128)(2,1)}, u32[]{:S(2)}, u32[]{:S(2)}) async-start(bf16[16,32,2944]{2,1,0:T(8,128)(2,1)} %shard_map.94), calls=%async_computation.2 | async-start | bytes 6029312 | tf_op jit(solution)/shard_map/all_to_all | solution.py:275
  140.0 43.2 %collective-permute-start.22 = (bf16[3,240,256]{2,1,0:T(8,128)(2,1)S(1)}, bf16[3,240,256]{2,1,0:T(8,128)(2,1)S(1)}, u32[]{:S(2)}, u32[]{:S(2)}) collective-permute-start(bf16[3,240,256]{2,1,0:T(8,128)(2,1)S(1)} %copy-done.18), channel_id=1, source_target_pairs={{0,128},{128,0},{1,129},{129,1},{2,130},{130,2},{3,131},{131,3},{4... | collective-permute-start | bytes 1105928 | tf_op jit(solution)/shard_map/ppermute | solution.py:261
  142.8 9.6 %collective-permute-start.15 = (bf16[16,2880]{1,0:T(8,128)(2,1)S(1)}, bf16[16,2880]{1,0:T(8,128)(2,1)S(1)}, u32[]{:S(2)}, u32[]{:S(2)}) collective-permute-start(bf16[16,2880]{1,0:T(8,128)(2,1)S(1)} %get-tuple-element.47), channel_id=1, source_target_pairs={{0,112},{16,0},{32,16},{48,32},{64,48},{80,64},{96,80},{112,96},{1... | collective-permute-start | bytes 276488 | tf_op jit(solution)/shard_map/ppermute | solution.py:257
  145.6 9.1 %collective-permute-start.16 = (bf16[16,2880]{1,0:T(8,128)(2,1)S(1)}, bf16[16,2880]{1,0:T(8,128)(2,1)S(1)}, u32[]{:S(2)}, u32[]{:S(2)}) collective-permute-start(bf16[16,2880]{1,0:T(8,128)(2,1)S(1)} %get-tuple-element.48), channel_id=1, source_target_pairs={{0,96},{16,112},{32,0},{48,16},{64,32},{80,48},{96,64},{112,80},{1... | collective-permute-start | bytes 276488 | tf_op jit(solution)/shard_map/ppermute | solution.py:257
  147.3 14.5 %collective-permute-start.17 = (bf16[16,2880]{1,0:T(8,128)(2,1)S(1)}, bf16[16,2880]{1,0:T(8,128)(2,1)S(1)}, u32[]{:S(2)}, u32[]{:S(2)}) collective-permute-start(bf16[16,2880]{1,0:T(8,128)(2,1)S(1)} %get-tuple-element.49), channel_id=1, source_target_pairs={{0,80},{16,96},{32,112},{48,0},{64,16},{80,32},{96,48},{112,64},{1... | collective-permute-start | bytes 276488 | tf_op jit(solution)/shard_map/ppermute | solution.py:257
  148.2 17.1 %collective-permute-start.18 = (bf16[16,2880]{1,0:T(8,128)(2,1)S(1)}, bf16[16,2880]{1,0:T(8,128)(2,1)S(1)}, u32[]{:S(2)}, u32[]{:S(2)}) collective-permute-start(bf16[16,2880]{1,0:T(8,128)(2,1)S(1)} %get-tuple-element.50), channel_id=1, source_target_pairs={{0,64},{16,80},{32,96},{48,112},{64,0},{80,16},{96,32},{112,48},{1... | collective-permute-start | bytes 276488 | tf_op jit(solution)/shard_map/ppermute | solution.py:257
  152.4 13.9 %collective-permute-start.19 = (bf16[16,2880]{1,0:T(8,128)(2,1)S(1)}, bf16[16,2880]{1,0:T(8,128)(2,1)S(1)}, u32[]{:S(2)}, u32[]{:S(2)}) collective-permute-start(bf16[16,2880]{1,0:T(8,128)(2,1)S(1)} %get-tuple-element.51), channel_id=1, source_target_pairs={{0,48},{16,64},{32,80},{48,96},{64,112},{80,0},{96,16},{112,32},{1... | collective-permute-start | bytes 276488 | tf_op jit(solution)/shard_map/ppermute | solution.py:257
  154.7 12.1 %collective-permute-start.20 = (bf16[16,2880]{1,0:T(8,128)(2,1)S(1)}, bf16[16,2880]{1,0:T(8,128)(2,1)S(1)}, u32[]{:S(2)}, u32[]{:S(2)}) collective-permute-start(bf16[16,2880]{1,0:T(8,128)(2,1)S(1)} %get-tuple-element.52), channel_id=1, source_target_pairs={{0,32},{16,48},{32,64},{48,80},{64,96},{80,112},{96,0},{112,16},{1... | collective-permute-start | bytes 276488 | tf_op jit(solution)/shard_map/ppermute | solution.py:257
  (21 other events, 142.6 us)

commit v4 on v3

--- a/solution.py
+++ b/solution.py
@@ -329,7 +329,7 @@
         5 * row_flops * UNITS,
         14_000_000,
         [pltpu.VMEM((ROWS, WIDE), BF16)],
-        28,
+        40,
     )(limit, replica, pairs, slot_weights, far_sent)
     other = swap_dp(other)
 
@@ -351,7 +351,7 @@
         3 * row_flops * UNITS,
         12_000_000,
         [pltpu.VMEM((ROWS, WIDE), BF16)] * 2,
-        24,
+        40,
     )(own, other, pairs, far_pairs)
     grad_tokens = call(
         sum_kernel, shape((TOKENS, D)), [SMEM] + [VMEM] * (1 + PLANES), row_flops, 900_000

time: 191 us -> 189 us (0.990)
  local copies, waits for them, and re-layouts: 16.8 us -> 12.4 us
  Pallas kernels: 25.6 us -> 28.4 us
    unnamed x42 -> x40, local copies, waits for them, and re-layouts: 16.3 us -> 11.8 us
    pallas_call x1, Pallas kernels: 8.83 us -> 11.7 us  [shards(): call(unit_kernel, (shape((3, HALF, ROWS)), shape((3, HALF, ROWS)), shape(...]
where the time goes in v4:
time: 189 us
  starting transfers between devices  67.2 us (36%)
  waiting for transfers between devices  55.5 us (29%)
  Pallas kernels  28.4 us (15%)
  blocking collectives  24.6 us (13%)
  local copies, waits for them, and re-layouts  12.4 us (7%)
    ppermute x21, starting transfers between devices, along_z(): lax.ppermute(value, 'z', [(i, (i + by) % PLANES) for i in range(PLANES)])  50.1 us
    ppermute x21, waiting for transfers between devices, along_z(): lax.ppermute(value, 'z', [(i, (i + by) % PLANES) for i in range(PLANES)])  42.7 us
    all_to_all x1, blocking collectives, in_plane(): lax.all_to_all(blocks, PLANE, split_axis=0, concat_axis=0, tiled=True)  24.6 us
    ppermute x2, waiting for transfers between devices, swap_dp(): return lax.ppermute(value, 'dp', [(0, 1), (1, 0)])  12.8 us
    all_to_all x2, starting transfers between devices, in_plane(): lax.all_to_all(blocks, PLANE, split_axis=0, concat_axis=0, tiled=True)  11.9 us
    unnamed x40, local copies, waits for them, and re-layouts  11.8 us
    pallas_call x1, Pallas kernels, shards(): call(unit_kernel, (shape((3, HALF, ROWS)), shape((3, HALF, ROWS)), shape(...  11.7 us
    pallas_call x1, Pallas kernels, shards(): call(weight_kernel, shape((1, HALF, 3 * D)), [VMEM] * 4, 3 * row_flops *...  7.33 us
  transfers between devices with their start and end apart: 25, of which 15 were waited for; matrix products, arithmetic and copies ran while one was open for 0% of the time, Pallas kernels for 3%

profile of v4, /device:TPU:2, one launch (start us, length us, event | category | flops | bytes accessed | tf_op | source)
XLA Modules:
  0.0 188.9 jit_solution(10779384338534832428)
XLA Ops:
  4.0 3.3 %collective-permute-start.7 = (bf16[32,2944]{1,0:T(8,128)(2,1)S(1)}, bf16[32,2944]{1,0:T(8,128)(2,1)S(1)}, u32[]{:S(2)}, u32[]{:S(2)}) collective-permute-start(bf16[32,2944]{1,0:T(8,128)(2,1)S(1)} %shard_map.86.raw_ref), channel_id=1, source_target_pairs={{0,128},{128,0},{1,129},{129,1},{2,130},{130,2},{3,131},{131,3},{4... | collective-permute-start | bytes 565256 | tf_op jit(solution)/shard_map/ppermute | solution.py:261
  10.6 3.3 %collective-permute-start.1 = (bf16[24,2944]{1,0:T(8,128)(2,1)S(1)}, bf16[24,2944]{1,0:T(8,128)(2,1)S(1)}, u32[]{:S(2)}, u32[]{:S(2)}) collective-permute-start(bf16[24,2944]{1,0:T(8,128)(2,1)S(1)} %get-tuple-element.31), channel_id=1, source_target_pairs={{0,32},{16,48},{32,64},{48,80},{64,96},{80,112},{96,0},{112,16},{1... | collective-permute-start | bytes 423944 | tf_op jit(solution)/shard_map/ppermute | solution.py:257
  13.8 4.0 %collective-permute-start.2 = (bf16[24,2944]{1,0:T(8,128)(2,1)S(1)}, bf16[24,2944]{1,0:T(8,128)(2,1)S(1)}, u32[]{:S(2)}, u32[]{:S(2)}) collective-permute-start(bf16[24,2944]{1,0:T(8,128)(2,1)S(1)} %get-tuple-element.32), channel_id=1, source_target_pairs={{0,48},{16,64},{32,80},{48,96},{64,112},{80,0},{96,16},{112,32},{1... | collective-permute-start | bytes 423944 | tf_op jit(solution)/shard_map/ppermute | solution.py:257
  19.9 3.4 %collective-permute-start.4 = (bf16[24,2944]{1,0:T(8,128)(2,1)S(1)}, bf16[24,2944]{1,0:T(8,128)(2,1)S(1)}, u32[]{:S(2)}, u32[]{:S(2)}) collective-permute-start(bf16[24,2944]{1,0:T(8,128)(2,1)S(1)} %get-tuple-element.34), channel_id=1, source_target_pairs={{0,80},{16,96},{32,112},{48,0},{64,16},{80,32},{96,48},{112,64},{1... | collective-permute-start | bytes 423944 | tf_op jit(solution)/shard_map/ppermute | solution.py:257
  23.4 5.6 %collective-permute-done.1.refs_2_ = bf16[24,2944]{1,0:T(8,128)(2,1)S(1)} collective-permute-done((bf16[24,2944]{1,0:T(8,128)(2,1)S(1)}, bf16[24,2944]{1,0:T(8,128)(2,1)S(1)}, u32[]{:S(2)}, u32[]{:S(2)}) %collective-permute-start.1) | collective-permute-done | bytes 141344 | tf_op jit(solution)/shard_map/ppermute | solution.py:257
  29.5 3.8 %collective-permute-start.6 = (bf16[24,2944]{1,0:T(8,128)(2,1)S(1)}, bf16[24,2944]{1,0:T(8,128)(2,1)S(1)}, u32[]{:S(2)}, u32[]{:S(2)}) collective-permute-start(bf16[24,2944]{1,0:T(8,128)(2,1)S(1)} %get-tuple-element.36), channel_id=1, source_target_pairs={{0,112},{16,0},{32,16},{48,32},{64,48},{80,64},{96,80},{112,96},{1... | collective-permute-start | bytes 423944 | tf_op jit(solution)/shard_map/ppermute | solution.py:257
  36.9 3.0 %collective-permute-done.4.refs_5_ = bf16[24,2944]{1,0:T(8,128)(2,1)S(1)} collective-permute-done((bf16[24,2944]{1,0:T(8,128)(2,1)S(1)}, bf16[24,2944]{1,0:T(8,128)(2,1)S(1)}, u32[]{:S(2)}, u32[]{:S(2)}) %collective-permute-start.4) | collective-permute-done | bytes 141344 | tf_op jit(solution)/shard_map/ppermute | solution.py:257
  39.9 3.0 %collective-permute-done.5.refs_6_ = bf16[24,2944]{1,0:T(8,128)(2,1)S(1)} collective-permute-done((bf16[24,2944]{1,0:T(8,128)(2,1)S(1)}, bf16[24,2944]{1,0:T(8,128)(2,1)S(1)}, u32[]{:S(2)}, u32[]{:S(2)}) %collective-permute-start.5) | collective-permute-done | bytes 141344 | tf_op jit(solution)/shard_map/ppermute | solution.py:257
  45.2 3.3 %shard_map.89 = bf16[16,32,2944]{2,1,0:T(8,128)(2,1)} custom-call(s32[128]{0:T(128)S(1)} %copy-done.14, s32[1]{0:T(128)} %bitcast.plane_ref, bf16[24,2944]{1,0:T(8,128)(2,1)S(1)} %get-tuple-element.29.refs_0_, bf16[24,2944]{1,0:T(8,128)(2,1)S(1)} %collective-permute-done.refs_1_, bf16[24,2944]{1,0:T(8,128)(2,1)S(1)} %collective-permute-done.1.refs_2_, ...), custom_call_target="tpu_custom_call" | custom-call | flops 566231040 | bytes 4200000 | tf_op jit(solution)/shard_map/pallas_call | solution.py:310
  48.5 5.1 %all-to-all-start = ((bf16[16,32,2944]{2,1,0:T(8,128)(2,1)}), bf16[16,32,2944]{2,1,0:T(8,128)(2,1)}, u32[]{:S(2)}, u32[]{:S(2)}) async-start(bf16[16,32,2944]{2,1,0:T(8,128)(2,1)} %shard_map.89), calls=%async_computation | async-start | bytes 6029312 | tf_op jit(solution)/shard_map/all_to_all | solution.py:275
  53.6 2.9 %collective-permute-start.8 = (bf16[24,2944]{1,0:T(8,128)(2,1)S(1)}, bf16[24,2944]{1,0:T(8,128)(2,1)S(1)}, u32[]{:S(2)}, u32[]{:S(2)}) collective-permute-start(bf16[24,2944]{1,0:T(8,128)(2,1)S(1)} %get-tuple-element.38), channel_id=1, source_target_pairs={{0,16},{16,32},{32,48},{48,64},{64,80},{80,96},{96,112},{112,0},{1... | collective-permute-start | bytes 423944 | tf_op jit(solution)/shard_map/ppermute | solution.py:257
  58.2 4.7 %collective-permute-start.11 = (bf16[24,2944]{1,0:T(8,128)(2,1)S(1)}, bf16[24,2944]{1,0:T(8,128)(2,1)S(1)}, u32[]{:S(2)}, u32[]{:S(2)}) collective-permute-start(bf16[24,2944]{1,0:T(8,128)(2,1)S(1)} %get-tuple-element.41), channel_id=1, source_target_pairs={{0,64},{16,80},{32,96},{48,112},{64,0},{80,16},{96,32},{112,48},{1... | collective-permute-start | bytes 423944 | tf_op jit(solution)/shard_map/ppermute | solution.py:257
  66.8 7.9 %collective-permute-done.9.refs_2_ = bf16[24,2944]{1,0:T(8,128)(2,1)S(1)} collective-permute-done((bf16[24,2944]{1,0:T(8,128)(2,1)S(1)}, bf16[24,2944]{1,0:T(8,128)(2,1)S(1)}, u32[]{:S(2)}, u32[]{:S(2)}) %collective-permute-start.9) | collective-permute-done | bytes 141344 | tf_op jit(solution)/shard_map/ppermute | solution.py:257
  76.0 3.9 %collective-permute-done.11.refs_4_ = bf16[24,2944]{1,0:T(8,128)(2,1)S(1)} collective-permute-done((bf16[24,2944]{1,0:T(8,128)(2,1)S(1)}, bf16[24,2944]{1,0:T(8,128)(2,1)S(1)}, u32[]{:S(2)}, u32[]{:S(2)}) %collective-permute-start.11) | collective-permute-done | bytes 141344 | tf_op jit(solution)/shard_map/ppermute | solution.py:257
  81.2 4.2 %collective-permute-done.13.refs_6_ = bf16[24,2944]{1,0:T(8,128)(2,1)S(1)} collective-permute-done((bf16[24,2944]{1,0:T(8,128)(2,1)S(1)}, bf16[24,2944]{1,0:T(8,128)(2,1)S(1)}, u32[]{:S(2)}, u32[]{:S(2)}) %collective-permute-start.13) | collective-permute-done | bytes 141344 | tf_op jit(solution)/shard_map/ppermute | solution.py:257
  95.2 11.7 %shard_map.91 = (bf16[3,240,256]{2,1,0:T(8,128)(2,1)S(1)}, bf16[3,240,256]{2,1,0:T(8,128)(2,1)S(1)}, bf16[256,2880]{1,0:T(8,128)(2,1)S(1)}) custom-call(s32[1]{0:T(128)} %dynamic_slice.3.limit_ref, s32[1]{0:T(128)} %bitcast.1.replica_ref, bf16[16,32,2944]{2,1,0:T(8,128)(2,1)} %all-to-all-done.pair_ref, bf16[480,8640]{1,0:T(8,128)(2,1)} %bitcast.8, ...), custom_call_target="tpu_custom_call" | custom-call | flops 3538944000 | bytes 14000000 | tf_op jit(solution)/shard_map/pallas_call | solution.py:325
  106.9 24.6 %all_to_all.15 = bf16[16,16,2880]{2,1,0:T(8,128)(2,1)} all-to-all(bf16[16,16,2880]{2,1,0:T(8,128)(2,1)S(1)} %bitcast.7), channel_id=1, replica_groups=mesh['dp'=2,'z'=8,'x'=4,'y'=2,'c'=2] {'x','y','c'}, dimensions={0} | all-to-all | bytes 2949120 | tf_op jit(solution)/shard_map/all_to_all | solution.py:275
  131.5 6.8 %all-to-all-start.2 = ((bf16[16,32,2944]{2,1,0:T(8,128)(2,1)}), bf16[16,32,2944]{2,1,0:T(8,128)(2,1)}, u32[]{:S(2)}, u32[]{:S(2)}) async-start(bf16[16,32,2944]{2,1,0:T(8,128)(2,1)} %shard_map.94), calls=%async_computation.2 | async-start | bytes 6029312 | tf_op jit(solution)/shard_map/all_to_all | solution.py:275
  146.6 4.2 %collective-permute-start.18 = (bf16[16,2880]{1,0:T(8,128)(2,1)S(1)}, bf16[16,2880]{1,0:T(8,128)(2,1)S(1)}, u32[]{:S(2)}, u32[]{:S(2)}) collective-permute-start(bf16[16,2880]{1,0:T(8,128)(2,1)S(1)} %get-tuple-element.50), channel_id=1, source_target_pairs={{0,64},{16,80},{32,96},{48,112},{64,0},{80,16},{96,32},{112,48},{1... | collective-permute-start | bytes 276488 | tf_op jit(solution)/shard_map/ppermute | solution.py:257
  153.0 3.9 %collective-permute-start.20 = (bf16[16,2880]{1,0:T(8,128)(2,1)S(1)}, bf16[16,2880]{1,0:T(8,128)(2,1)S(1)}, u32[]{:S(2)}, u32[]{:S(2)}) collective-permute-start(bf16[16,2880]{1,0:T(8,128)(2,1)S(1)} %get-tuple-element.52), channel_id=1, source_target_pairs={{0,32},{16,48},{32,64},{48,80},{64,96},{80,112},{96,0},{112,16},{1... | collective-permute-start | bytes 276488 | tf_op jit(solution)/shard_map/ppermute | solution.py:257
  156.9 3.2 %collective-permute-done.17.refs_3_ = bf16[16,2880]{1,0:T(8,128)(2,1)S(1)} collective-permute-done((bf16[16,2880]{1,0:T(8,128)(2,1)S(1)}, bf16[16,2880]{1,0:T(8,128)(2,1)S(1)}, u32[]{:S(2)}, u32[]{:S(2)}) %collective-permute-start.17) | collective-permute-done | bytes 92192 | tf_op jit(solution)/shard_map/ppermute | solution.py:257
  160.2 3.5 %collective-permute-start.21 = (bf16[16,2880]{1,0:T(8,128)(2,1)S(1)}, bf16[16,2880]{1,0:T(8,128)(2,1)S(1)}, u32[]{:S(2)}, u32[]{:S(2)}) collective-permute-start(bf16[16,2880]{1,0:T(8,128)(2,1)S(1)} %get-tuple-element.53), channel_id=1, source_target_pairs={{0,16},{16,32},{32,48},{48,64},{64,80},{80,96},{96,112},{112,0},{1... | collective-permute-start | bytes 276488 | tf_op jit(solution)/shard_map/ppermute | solution.py:257
  168.8 12.8 %collective-permute-done.22.other_ref = bf16[3,240,256]{2,1,0:T(8,128)(2,1)S(1)} collective-permute-done((bf16[3,240,256]{2,1,0:T(8,128)(2,1)S(1)}, bf16[3,240,256]{2,1,0:T(8,128)(2,1)S(1)}, u32[]{:S(2)}, u32[]{:S(2)}) %collective-permute-start.22) | collective-permute-done | bytes 368672 | tf_op jit(solution)/shard_map/ppermute | solution.py:261
  181.6 7.3 %shard_map.95 = bf16[1,240,8640]{2,1,0:T(8,128)(2,1)} custom-call(bf16[3,240,256]{2,1,0:T(8,128)(2,1)S(1)} %get-tuple-element.54.own_ref, bf16[3,240,256]{2,1,0:T(8,128)(2,1)S(1)} %collective-permute-done.22.other_ref, bf16[16,32,2944]{2,1,0:T(8,128)(2,1)} %all-to-all-done.pair_ref, bf16[16,32,2944]{2,1,0:T(8,128)(2,1)} %all-to-all-done.2.far_ref), custom_call_target="tpu_custom_call" | custom-call | flops 2123366400 | bytes 12000000 | tf_op jit(solution)/shard_map/pallas_call | solution.py:347
  (78 shorter events, 48.7 us)
Async XLA Ops:
  4.0 25.5 %collective-permute-start.7 = (bf16[32,2944]{1,0:T(8,128)(2,1)S(1)}, bf16[32,2944]{1,0:T(8,128)(2,1)S(1)}, u32[]{:S(2)}, u32[]{:S(2)}) collective-permute-start(bf16[32,2944]{1,0:T(8,128)(2,1)S(1)} %shard_map.86.raw_ref), channel_id=1, source_target_pairs={{0,128},{128,0},{1,129},{129,1},{2,130},{130,2},{3,131},{131,3},{4... | collective-permute-start | bytes 565256 | tf_op jit(solution)/shard_map/ppermute | solution.py:261
  8.6 11.4 %collective-permute-start = (bf16[24,2944]{1,0:T(8,128)(2,1)S(1)}, bf16[24,2944]{1,0:T(8,128)(2,1)S(1)}, u32[]{:S(2)}, u32[]{:S(2)}) collective-permute-start(bf16[24,2944]{1,0:T(8,128)(2,1)S(1)} %get-tuple-element.30), channel_id=1, source_target_pairs={{0,16},{16,32},{32,48},{48,64},{64,80},{80,96},{96,112},{112,0},{1... | collective-permute-start | bytes 423944 | tf_op jit(solution)/shard_map/ppermute | solution.py:257
  10.6 18.4 %collective-permute-start.1 = (bf16[24,2944]{1,0:T(8,128)(2,1)S(1)}, bf16[24,2944]{1,0:T(8,128)(2,1)S(1)}, u32[]{:S(2)}, u32[]{:S(2)}) collective-permute-start(bf16[24,2944]{1,0:T(8,128)(2,1)S(1)} %get-tuple-element.31), channel_id=1, source_target_pairs={{0,32},{16,48},{32,64},{48,80},{64,96},{80,112},{96,0},{112,16},{1... | collective-permute-start | bytes 423944 | tf_op jit(solution)/shard_map/ppermute | solution.py:257
  13.8 23.1 %collective-permute-start.2 = (bf16[24,2944]{1,0:T(8,128)(2,1)S(1)}, bf16[24,2944]{1,0:T(8,128)(2,1)S(1)}, u32[]{:S(2)}, u32[]{:S(2)}) collective-permute-start(bf16[24,2944]{1,0:T(8,128)(2,1)S(1)} %get-tuple-element.32), channel_id=1, source_target_pairs={{0,48},{16,64},{32,80},{48,96},{64,112},{80,0},{96,16},{112,32},{1... | collective-permute-start | bytes 423944 | tf_op jit(solution)/shard_map/ppermute | solution.py:257
  17.9 19.0 %collective-permute-start.3 = (bf16[24,2944]{1,0:T(8,128)(2,1)S(1)}, bf16[24,2944]{1,0:T(8,128)(2,1)S(1)}, u32[]{:S(2)}, u32[]{:S(2)}) collective-permute-start(bf16[24,2944]{1,0:T(8,128)(2,1)S(1)} %get-tuple-element.33), channel_id=1, source_target_pairs={{0,64},{16,80},{32,96},{48,112},{64,0},{80,16},{96,32},{112,48},{1... | collective-permute-start | bytes 423944 | tf_op jit(solution)/shard_map/ppermute | solution.py:257
  19.9 19.9 %collective-permute-start.4 = (bf16[24,2944]{1,0:T(8,128)(2,1)S(1)}, bf16[24,2944]{1,0:T(8,128)(2,1)S(1)}, u32[]{:S(2)}, u32[]{:S(2)}) collective-permute-start(bf16[24,2944]{1,0:T(8,128)(2,1)S(1)} %get-tuple-element.34), channel_id=1, source_target_pairs={{0,80},{16,96},{32,112},{48,0},{64,16},{80,32},{96,48},{112,64},{1... | collective-permute-start | bytes 423944 | tf_op jit(solution)/shard_map/ppermute | solution.py:257
  28.9 13.9 %collective-permute-start.5 = (bf16[24,2944]{1,0:T(8,128)(2,1)S(1)}, bf16[24,2944]{1,0:T(8,128)(2,1)S(1)}, u32[]{:S(2)}, u32[]{:S(2)}) collective-permute-start(bf16[24,2944]{1,0:T(8,128)(2,1)S(1)} %get-tuple-element.35), channel_id=1, source_target_pairs={{0,96},{16,112},{32,0},{48,16},{64,32},{80,48},{96,64},{112,80},{1... | collective-permute-start | bytes 423944 | tf_op jit(solution)/shard_map/ppermute | solution.py:257
  29.5 15.0 %collective-permute-start.6 = (bf16[24,2944]{1,0:T(8,128)(2,1)S(1)}, bf16[24,2944]{1,0:T(8,128)(2,1)S(1)}, u32[]{:S(2)}, u32[]{:S(2)}) collective-permute-start(bf16[24,2944]{1,0:T(8,128)(2,1)S(1)} %get-tuple-element.36), channel_id=1, source_target_pairs={{0,112},{16,0},{32,16},{48,32},{64,48},{80,64},{96,80},{112,96},{1... | collective-permute-start | bytes 423944 | tf_op jit(solution)/shard_map/ppermute | solution.py:257
  48.5 46.7 %all-to-all-start = ((bf16[16,32,2944]{2,1,0:T(8,128)(2,1)}), bf16[16,32,2944]{2,1,0:T(8,128)(2,1)}, u32[]{:S(2)}, u32[]{:S(2)}) async-start(bf16[16,32,2944]{2,1,0:T(8,128)(2,1)} %shard_map.89), calls=%async_computation | async-start | bytes 6029312 | tf_op jit(solution)/shard_map/all_to_all | solution.py:275
  53.6 11.5 %collective-permute-start.8 = (bf16[24,2944]{1,0:T(8,128)(2,1)S(1)}, bf16[24,2944]{1,0:T(8,128)(2,1)S(1)}, u32[]{:S(2)}, u32[]{:S(2)}) collective-permute-start(bf16[24,2944]{1,0:T(8,128)(2,1)S(1)} %get-tuple-element.38), channel_id=1, source_target_pairs={{0,16},{16,32},{32,48},{48,64},{64,80},{80,96},{96,112},{112,0},{1... | collective-permute-start | bytes 423944 | tf_op jit(solution)/shard_map/ppermute | solution.py:257
  56.5 18.3 %collective-permute-start.9 = (bf16[24,2944]{1,0:T(8,128)(2,1)S(1)}, bf16[24,2944]{1,0:T(8,128)(2,1)S(1)}, u32[]{:S(2)}, u32[]{:S(2)}) collective-permute-start(bf16[24,2944]{1,0:T(8,128)(2,1)S(1)} %get-tuple-element.39), channel_id=1, source_target_pairs={{0,32},{16,48},{32,64},{48,80},{64,96},{80,112},{96,0},{112,16},{1... | collective-permute-start | bytes 423944 | tf_op jit(solution)/shard_map/ppermute | solution.py:257
  57.6 17.7 %collective-permute-start.10 = (bf16[24,2944]{1,0:T(8,128)(2,1)S(1)}, bf16[24,2944]{1,0:T(8,128)(2,1)S(1)}, u32[]{:S(2)}, u32[]{:S(2)}) collective-permute-start(bf16[24,2944]{1,0:T(8,128)(2,1)S(1)} %get-tuple-element.40), channel_id=1, source_target_pairs={{0,48},{16,64},{32,80},{48,96},{64,112},{80,0},{96,16},{112,32},{1... | collective-permute-start | bytes 423944 | tf_op jit(solution)/shard_map/ppermute | solution.py:257
  58.2 21.7 %collective-permute-start.11 = (bf16[24,2944]{1,0:T(8,128)(2,1)S(1)}, bf16[24,2944]{1,0:T(8,128)(2,1)S(1)}, u32[]{:S(2)}, u32[]{:S(2)}) collective-permute-start(bf16[24,2944]{1,0:T(8,128)(2,1)S(1)} %get-tuple-element.41), channel_id=1, source_target_pairs={{0,64},{16,80},{32,96},{48,112},{64,0},{80,16},{96,32},{112,48},{1... | collective-permute-start | bytes 423944 | tf_op jit(solution)/shard_map/ppermute | solution.py:257
  62.9 17.6 %collective-permute-start.12 = (bf16[24,2944]{1,0:T(8,128)(2,1)S(1)}, bf16[24,2944]{1,0:T(8,128)(2,1)S(1)}, u32[]{:S(2)}, u32[]{:S(2)}) collective-permute-start(bf16[24,2944]{1,0:T(8,128)(2,1)S(1)} %get-tuple-element.42), channel_id=1, source_target_pairs={{0,80},{16,96},{32,112},{48,0},{64,16},{80,32},{96,48},{112,64},{1... | collective-permute-start | bytes 423944 | tf_op jit(solution)/shard_map/ppermute | solution.py:257
  65.1 20.3 %collective-permute-start.13 = (bf16[24,2944]{1,0:T(8,128)(2,1)S(1)}, bf16[24,2944]{1,0:T(8,128)(2,1)S(1)}, u32[]{:S(2)}, u32[]{:S(2)}) collective-permute-start(bf16[24,2944]{1,0:T(8,128)(2,1)S(1)} %get-tuple-element.43), channel_id=1, source_target_pairs={{0,96},{16,112},{32,0},{48,16},{64,32},{80,48},{96,64},{112,80},{1... | collective-permute-start | bytes 423944 | tf_op jit(solution)/shard_map/ppermute | solution.py:257
  74.8 13.5 %collective-permute-start.14 = (bf16[24,2944]{1,0:T(8,128)(2,1)S(1)}, bf16[24,2944]{1,0:T(8,128)(2,1)S(1)}, u32[]{:S(2)}, u32[]{:S(2)}) collective-permute-start(bf16[24,2944]{1,0:T(8,128)(2,1)S(1)} %get-tuple-element.44), channel_id=1, source_target_pairs={{0,112},{16,0},{32,16},{48,32},{64,48},{80,64},{96,80},{112,96},{1... | collective-permute-start | bytes 423944 | tf_op jit(solution)/shard_map/ppermute | solution.py:257
  131.5 50.1 %all-to-all-start.2 = ((bf16[16,32,2944]{2,1,0:T(8,128)(2,1)}), bf16[16,32,2944]{2,1,0:T(8,128)(2,1)}, u32[]{:S(2)}, u32[]{:S(2)}) async-start(bf16[16,32,2944]{2,1,0:T(8,128)(2,1)} %shard_map.94), calls=%async_computation.2 | async-start | bytes 6029312 | tf_op jit(solution)/shard_map/all_to_all | solution.py:275
  138.3 43.2 %collective-permute-start.22 = (bf16[3,240,256]{2,1,0:T(8,128)(2,1)S(1)}, bf16[3,240,256]{2,1,0:T(8,128)(2,1)S(1)}, u32[]{:S(2)}, u32[]{:S(2)}) collective-permute-start(bf16[3,240,256]{2,1,0:T(8,128)(2,1)S(1)} %copy-done.17), channel_id=1, source_target_pairs={{0,128},{128,0},{1,129},{129,1},{2,130},{130,2},{3,131},{131,3},{4... | collective-permute-start | bytes 1105928 | tf_op jit(solution)/shard_map/ppermute | solution.py:261
  141.2 9.6 %collective-permute-start.15 = (bf16[16,2880]{1,0:T(8,128)(2,1)S(1)}, bf16[16,2880]{1,0:T(8,128)(2,1)S(1)}, u32[]{:S(2)}, u32[]{:S(2)}) collective-permute-start(bf16[16,2880]{1,0:T(8,128)(2,1)S(1)} %get-tuple-element.47), channel_id=1, source_target_pairs={{0,112},{16,0},{32,16},{48,32},{64,48},{80,64},{96,80},{112,96},{1... | collective-permute-start | bytes 276488 | tf_op jit(solution)/shard_map/ppermute | solution.py:257
  143.9 9.1 %collective-permute-start.16 = (bf16[16,2880]{1,0:T(8,128)(2,1)S(1)}, bf16[16,2880]{1,0:T(8,128)(2,1)S(1)}, u32[]{:S(2)}, u32[]{:S(2)}) collective-permute-start(bf16[16,2880]{1,0:T(8,128)(2,1)S(1)} %get-tuple-element.48), channel_id=1, source_target_pairs={{0,96},{16,112},{32,0},{48,16},{64,32},{80,48},{96,64},{112,80},{1... | collective-permute-start | bytes 276488 | tf_op jit(solution)/shard_map/ppermute | solution.py:257
  145.7 14.5 %collective-permute-start.17 = (bf16[16,2880]{1,0:T(8,128)(2,1)S(1)}, bf16[16,2880]{1,0:T(8,128)(2,1)S(1)}, u32[]{:S(2)}, u32[]{:S(2)}) collective-permute-start(bf16[16,2880]{1,0:T(8,128)(2,1)S(1)} %get-tuple-element.49), channel_id=1, source_target_pairs={{0,80},{16,96},{32,112},{48,0},{64,16},{80,32},{96,48},{112,64},{1... | collective-permute-start | bytes 276488 | tf_op jit(solution)/shard_map/ppermute | solution.py:257
  146.6 17.1 %collective-permute-start.18 = (bf16[16,2880]{1,0:T(8,128)(2,1)S(1)}, bf16[16,2880]{1,0:T(8,128)(2,1)S(1)}, u32[]{:S(2)}, u32[]{:S(2)}) collective-permute-start(bf16[16,2880]{1,0:T(8,128)(2,1)S(1)} %get-tuple-element.50), channel_id=1, source_target_pairs={{0,64},{16,80},{32,96},{48,112},{64,0},{80,16},{96,32},{112,48},{1... | collective-permute-start | bytes 276488 | tf_op jit(solution)/shard_map/ppermute | solution.py:257
  150.8 13.9 %collective-permute-start.19 = (bf16[16,2880]{1,0:T(8,128)(2,1)S(1)}, bf16[16,2880]{1,0:T(8,128)(2,1)S(1)}, u32[]{:S(2)}, u32[]{:S(2)}) collective-permute-start(bf16[16,2880]{1,0:T(8,128)(2,1)S(1)} %get-tuple-element.51), channel_id=1, source_target_pairs={{0,48},{16,64},{32,80},{48,96},{64,112},{80,0},{96,16},{112,32},{1... | collective-permute-start | bytes 276488 | tf_op jit(solution)/shard_map/ppermute | solution.py:257
  153.0 12.1 %collective-permute-start.20 = (bf16[16,2880]{1,0:T(8,128)(2,1)S(1)}, bf16[16,2880]{1,0:T(8,128)(2,1)S(1)}, u32[]{:S(2)}, u32[]{:S(2)}) collective-permute-start(bf16[16,2880]{1,0:T(8,128)(2,1)S(1)} %get-tuple-element.52), channel_id=1, source_target_pairs={{0,32},{16,48},{32,64},{48,80},{64,96},{80,112},{96,0},{112,16},{1... | collective-permute-start | bytes 276488 | tf_op jit(solution)/shard_map/ppermute | solution.py:257
  (20 other events, 136.5 us)
